TPU v7x, 256 devices: a whole 4x4x8 slice. The times are simulated.
256 devices in a mesh: sp: 32 (over y, z_lo, x), op: 8 (over z_hi, core).
Axes of the slice: x: 4, y: 4, z: 8 (z_hi: 4, z_lo: 2; z = z_hi * 2 + z_lo), core: 2. Of those that a mesh axis runs over, the one named last changes fastest.
Arguments:
- amplitudes: bfloat16 [256, 1408, 1408], P('op', 'sp'), may hold values from -6 to 6
- window_coef: bfloat16 [12, 1408], replicated, may hold values from -0.4375 to 0.4375
- virtual_coef: bfloat16 [2048, 1408], P(None, 'sp'), may hold values from -0.15625 to 0.15625
- integrals: bfloat16 [24576, 24576], P('sp', 'op'), may hold values from -0.0390625 to 0.0390625
- block_mask: int32 [96, 96], P('sp', 'op'), may hold values 0 or 1
Outputs:
- ladder_out: bfloat16 [256, 1408, 1408], P('op', 'sp')
All inputs are finite; a program needn't handle non-finite values. No bound on the sum of `block_mask` on one device may be relied on, other than what follows from the above.
Results may differ from a plain program's by a relative error of at most 0.013.
Values may be sent and summed in bfloat16 or wider, within the bound.
No kernel may reach another device: no remote copies, remote signals or barrier semaphores. Data moves between devices by JAX's collectives and lax.ppermute only.
A program may use at most 128 MiB of HBM per device.

v0:
```python
import jax
import jax.numpy as jnp
from jax import lax
from jax.sharding import PartitionSpec as P

NAO = 2048
NUW = 12
NPAIR = 24576


def local(amplitudes, window_coef, virtual_coef, integrals, block_mask):
    own_pairs = amplitudes.shape[0]
    half = jnp.einsum(
        "pab,nb->pan", amplitudes, window_coef, preferred_element_type=jnp.float32
    ).astype(jnp.bfloat16)
    partial_amp = jnp.einsum("ma,pan->pmn", virtual_coef, half, preferred_element_type=jnp.float32)
    partial_amp = partial_amp.reshape(own_pairs, NPAIR)
    ao_amp = lax.psum_scatter(partial_amp, "sp", scatter_dimension=1, tiled=True).astype(
        jnp.bfloat16
    )
    all_amp = lax.all_gather(ao_amp, "op", axis=0, tiled=True)
    in_rows, out_cols = integrals.shape
    mask_rows, mask_cols = block_mask.shape
    row_block = in_rows // mask_rows
    col_block = out_cols // mask_cols
    keep = block_mask.astype(integrals.dtype)[:, None, :, None]
    screened = (integrals.reshape(mask_rows, row_block, mask_cols, col_block) * keep).reshape(
        in_rows, out_cols
    )
    terms = jnp.dot(all_amp, screened, preferred_element_type=jnp.float32)
    ladder = lax.psum(terms, "sp").astype(jnp.bfloat16)
    owned = lax.all_to_all(ladder, "op", split_axis=0, concat_axis=1, tiled=True)
    owned = owned.reshape(own_pairs, NAO, NUW)
    forward = jnp.einsum(
        "ma,pmn->pan", virtual_coef, owned, preferred_element_type=jnp.float32
    ).astype(jnp.bfloat16)
    return jnp.einsum(
        "pan,nb->pab", forward, window_coef, preferred_element_type=jnp.float32
    ).astype(jnp.bfloat16)


def solution(mesh):
    placed = (P("op", "sp", None), P(), P(None, "sp"), P("sp", "op"), P("sp", "op"))
    return jax.shard_map(
        local, mesh=mesh, in_specs=placed, out_specs=P("op", "sp", None), check_vma=False
    )
```

profile of v0, /device:TPU:2, one launch (start us, length us, event | category | flops | bytes accessed | tf_op | source)
XLA Modules:
  0.0 490.1 jit_solution(14031557107995241814)
XLA Ops:
  6.5 0.0 copy-start
  6.5 0.0 reduce-scatter.2.cloned.1.call-start
  6.5 5.1 %convolution_convert_fusion.1 = bf16[32,44,12]{0,2,1:T(8,128)(2,1)S(1)} fusion(bf16[32,44,1408]{2,0,1:T(8,128)(2,1)} %param.5, bf16[12,1408]{1,0:T(8,128)(2,1)} %param.6), kind=kOutput, calls=%fused_computation.6 | convolution fusion | flops 47596032 | bytes 4032512 | tf_op jit(solution)/shard_map/pab,nb->pan/dot_general | solution.py:13
  11.6 0.0 copy-done
  11.6 0.6 convolution_bitcast_fusion
  12.2 11.2 %copy.18 = f32[32,2048,12]{0,2,1:T(8,128)} copy(f32[32,2048,12]{1,0,2:T(8,128)S(1)} %convolution_bitcast_fusion) | data formatting | bytes 6291456 | tf_op jit(solution)/shard_map/ma,pan->pmn/transpose | solution.py:16
  23.4 15.1 %reshape.14 = f32[32,24576]{0,1:T(8,128)} reshape(f32[32,2048,12]{0,2,1:T(8,128)} %copy.18) | data formatting | bytes 6291456 | tf_op jit(solution)/shard_map/reshape | solution.py:17
  38.6 0.0 copy-start.2
  38.6 8.8 %copy.19 = f32[32,24576]{1,0:T(8,128)} copy(f32[32,24576]{0,1:T(8,128)} %reshape.14) | data formatting | bytes 6291456 | tf_op jit(solution)/shard_map/reshape | solution.py:17
  47.4 0.0 reduce-scatter.2.cloned.1.call-update
  47.4 0.0 copy-done.2
  47.4 0.5 mul.11
  47.9 5.3 %copy.24 = bf16[96,8,12,256]{3,1,2,0:T(8,128)(2,1)} copy(bf16[96,8,12,256]{3,2,1,0:T(8,128)(2,1)S(1)} %bitcast.25) | data formatting | bytes 9437184
  53.2 160.5 %reduce-scatter.2.cloned.1.call-done = f32[32,768]{1,0:T(8,128)} async-done(((f32[32,24576]{1,0:T(8,128)}), f32[32,768]{1,0:T(8,128)}) %reduce-scatter.2.cloned.1.call-update) | async-done | bytes 98320 | tf_op jit(solution)/shard_map/reduce_scatter | solution.py:18
  213.7 0.9 convert_element_type.22
  214.6 16.6 %all_gather.3 = bf16[256,768]{1,0:T(8,128)(2,1)S(1)} all-gather(bf16[32,768]{1,0:T(8,128)(2,1)S(1)} %convert_element_type.22), channel_id=1, replica_groups=mesh['sp'=32,'op'=8] {'op'}, dimensions={0}, use_global_device_ids=true | all-gather | bytes 442368 | tf_op jit(solution)/shard_map/all_gather | solution.py:21
  231.2 5.2 %fusion.2 = f32[256,3072]{1,0:T(8,128)S(1)} fusion(bf16[256,768]{1,0:T(8,128)(2,1)S(1)} %all_gather.3, bf16[768,3072]{1,0:T(8,128)(2,1)} %param.8, bf16[768,3072]{1,0:T(8,128)(2,1)} %bitcast.26), kind=kOutput, calls=%fused_computation.2 | convolution fusion | flops 1210318848 | bytes 12976128 | tf_op jit(solution)/shard_map/dot_general | solution.py:30
  236.4 183.2 %all-reduce.1 = bf16[256,3072]{1,0:T(8,128)(2,1)} all-reduce(f32[256,3072]{1,0:T(8,128)S(1)} %fusion.2), channel_id=1, replica_groups=mesh['sp'=32,'op'=8] {'sp'}, use_global_device_ids=true, to_apply=%region_1.0 | all-reduce | flops 786432 | bytes 4718592 | tf_op jit(solution)/shard_map/psum | solution.py:31
  419.6 38.3 %all_to_all.16 = bf16[8,32,3072]{2,1,0:T(8,128)(2,1)S(1)} all-to-all(bf16[8,32,3072]{2,1,0:T(8,128)(2,1)} %bitcast.27), channel_id=1, replica_groups=mesh['sp'=32,'op'=8] {'op'}, dimensions={0} | all-to-all | bytes 3145728 | tf_op jit(solution)/shard_map/all_to_all | solution.py:32
  457.8 4.5 copy.20
  462.3 11.7 %reshape.15 = bf16[32,2048,12]{0,2,1:T(8,128)(2,1)} reshape(bf16[32,8,3072]{0,2,1:T(8,128)(2,1)} %copy.20) | data formatting | bytes 3145728 | tf_op jit(solution)/shard_map/reshape | solution.py:33
  474.0 0.0 copy-start.1
  474.0 5.2 %fusion.7 = bf16[32,44,12]{1,0,2:T(8,128)(2,1)S(1)} fusion(bf16[32,2048,12]{0,2,1:T(8,128)(2,1)} %reshape.15, bf16[2048,44]{0,1:T(8,128)(2,1)S(1)} %copy-done), kind=kOutput, calls=%fused_computation.8 | convolution fusion | flops 69222912 | bytes 1786880 | tf_op jit(solution)/shard_map/ma,pmn->pan/dot_general | solution.py:34
  479.2 0.0 copy-done.1
  479.2 1.4 convolution_convert_fusion
  480.6 2.7 copy.23
  (1 shorter events, 0.0 us)
Async XLA Ops:
  6.5 5.1 %copy-start = (bf16[2048,44]{0,1:T(8,128)(2,1)S(1)}, bf16[2048,44]{0,1:T(8,128)(2,1)}, u32[]{:S(2)}) copy-start(bf16[2048,44]{0,1:T(8,128)(2,1)} %param.7) | copy-start | bytes 540676
  6.5 207.2 %reduce-scatter.2.cloned.1.call-start = ((), (), s32[]{:S(2)}) async-start(), calls=%async_computation.2 | async-start | bytes 3244032 | tf_op jit(solution)/shard_map/reduce_scatter | solution.py:18
  38.6 8.8 %copy-start.2 = (s32[3,12]{1,0:T(4,128)S(1)}, s32[3,12]{1,0:T(4,128)}, u32[]{:S(2)}) copy-start(s32[3,12]{1,0:T(4,128)} %param.9) | copy-start | bytes 436
  474.0 5.2 %copy-start.1 = (bf16[12,1408]{1,0:T(8,128)(2,1)S(1)}, bf16[12,1408]{1,0:T(8,128)(2,1)}, u32[]{:S(2)}) copy-start(bf16[12,1408]{1,0:T(8,128)(2,1)} %param.6) | copy-start | bytes 101380
Sparse Core Ops, SparseCore 0:
  47.5 166.1 reduce-scatter.1
where the time goes:
time: 495 us; the launch traced here: 490 us
  blocking collectives  238 us (48%)
  waiting for transfers between devices  161 us (33%)
  local copies, waits for them, and re-layouts  59.8 us (12%)
  matrix products  17.4 us (4%)
  between operations  13.5 us (3%)
    psum x1, blocking collectives, local(): ladder = lax.psum(terms, 'sp').astype(jnp.bfloat16)  183 us
    reduce_scatter x1, waiting for transfers between devices, local(): lax.psum_scatter(partial_amp, 'sp', scatter_dimension=1, tiled=True)  161 us
    all_to_all x1, blocking collectives, local(): lax.all_to_all(ladder, 'op', split_axis=0, concat_axis=1, tiled=True)  38.3 us
    reshape x2, local copies, waits for them, and re-layouts, local(): partial_amp = partial_amp.reshape(own_pairs, NPAIR)  24 us
    all_gather x1, blocking collectives, local(): all_amp = lax.all_gather(ao_amp, 'op', axis=0, tiled=True)  16.6 us
    reshape x1, local copies, waits for them, and re-layouts, local(): owned = owned.reshape(own_pairs, NAO, NUW)  11.7 us
    transpose x1, local copies, waits for them, and re-layouts, local(): jnp.einsum('ma,pan->pmn', virtual_coef, half, preferred_element_type=jnp....  11.2 us
  transfers between devices with their start and end apart: 1, of which 1 were waited for; matrix products, arithmetic and copies ran while one was open for 1% of the time, Pallas kernels for 0%

commit v1 on v0

v1 whole, which is shorter than its diff:
```python
import functools

import jax
import jax.numpy as jnp
from jax import lax
from jax.experimental import pallas as pl
from jax.experimental.pallas import tpu as pltpu
from jax.sharding import Mesh
from jax.sharding import PartitionSpec as P

F32 = jnp.float32
BF16 = jnp.bfloat16
ROWS = (((0,), (0,)), ((), ()))
LANES = (((1,), (1,)), ((), ()))


def iota(shape, dim):
    return lax.broadcasted_iota(jnp.int32, shape, dim)


def div(x, n):
    if n & (n - 1) == 0:
        return lax.shift_right_logical(x, n.bit_length() - 1)
    return lax.shift_right_logical(x * ((1 << 19) // n + 1), 19)


def mod(x, n):
    return x & (n - 1) if n & (n - 1) == 0 else x - div(x, n) * n


def row_ids(size):
    return iota((size, 1), 0)


def lane_ids(size):
    return iota((1, size), 1)


def ones_where(cond):
    return jnp.where(cond, 1.0, 0.0).astype(BF16)


def mm(x, y):
    return jnp.dot(x, y, preferred_element_type=F32)


def half_kernel(
    steps, few, core_ref, amp_hbm, win_hbm, coef_hbm, out_ref, amp_ref, win_ref, coef_ref, sems
):
    total, pairs, _ = amp_hbm.shape
    nuw = win_hbm.shape[0]
    dests, padded, lanes = out_ref.shape
    side, squares, width = 4, 2, 128
    mus = lanes - width
    virt = total // steps
    rows = virt * pairs
    copies = [
        pltpu.make_async_copy(
            amp_hbm.at[step * virt : (step + 1) * virt],
            amp_ref.at[step * virt : (step + 1) * virt],
            sems.at[step],
        )
        for step in range(steps)
    ]
    count = coef_ref.shape[1]
    start = pl.multiple_of(core_ref[0] * count, count)
    win_copy = pltpu.make_async_copy(win_hbm, win_ref, sems.at[steps])
    coef_copy = pltpu.make_async_copy(coef_hbm.at[:, pl.ds(start, count)], coef_ref, sems.at[steps + 1])
    win_copy.start()
    coef_copy.start()
    for copy in copies[:2]:
        copy.start()
    coef_copy.wait()
    coef = coef_ref[...].astype(F32)
    run = mus // (count // (2 * mus))
    blocks = mus // run
    for x in range(side):
        for z in range(squares):
            at = (x * squares + z) * run
            chunk = [coef[:, b * 2 * mus + at : b * 2 * mus + at + run] for b in range(blocks)]
            chunk = jnp.concatenate(chunk, axis=1).astype(BF16)
            for y in range(side):
                dest = (y * squares + z) * side + x
                out_ref[dest, :, :mus] = jnp.zeros((padded, mus), BF16)
                out_ref[dest, :total, :mus] = chunk
    win_copy.wait()
    lane = row_ids(side * width)
    spread = ones_where(div(mod(lane, width), few) == lane_ids(nuw))
    pair_of = div(lane, width) * few + mod(lane, few)
    own = pair_of == mod(lane_ids(rows), pairs)
    gathered = None
    for step in range(steps):
        copies[step].wait()
        if step + 2 < steps:
            copies[step + 2].start()
        block = amp_ref[step * virt : (step + 1) * virt].reshape(rows, amp_ref.shape[2])
        half = lax.dot_general(win_ref[...], block, LANES, preferred_element_type=F32)
        wide = jnp.where(own, mm(spread, half.astype(BF16)), 0.0).astype(BF16)
        collect = ones_where(div(lane_ids(rows), pairs) + step * virt == row_ids(padded))
        part = lax.dot_general(collect, wide, LANES, preferred_element_type=F32)
        gathered = part if gathered is None else gathered + part
    gathered = gathered.astype(BF16)
    for y in range(side):
        for low in range(dests // side):
            out_ref[y * (dests // side) + low, :, mus:] = gathered[:, y * width : (y + 1) * width]


def amp_kernel(nuw, core_ref, in_ref, coef_ref, out_ref):
    parts, padded, lanes = in_ref.shape
    dests, few, cols = out_ref.shape
    width = 128
    mus = lanes - width
    half = in_ref[:, :, mus:].reshape(parts * padded, width)
    every = mus * nuw
    repeat = dests * cols // (2 * every)
    blocks = dests // (2 * repeat)
    rows_of = ones_where(div(row_ids(every), nuw) == lane_ids(mus))
    own = mod(row_ids(every), nuw) == div(lane_ids(width), few)
    pick = ones_where(row_ids(2 * few) == mod(lane_ids(width), few))
    for other in range(2):
        coef = coef_ref[...] if other else in_ref[:, :, :mus]
        coef = coef.reshape(parts * padded, mus)
        amp = lax.dot_general(coef, half, ROWS, preferred_element_type=F32).astype(BF16)
        wide = jnp.where(own, mm(rows_of, amp), 0.0).astype(BF16)
        ordered = lax.dot_general(pick, wide, LANES, preferred_element_type=F32)[:few].astype(BF16)
        for b in range(blocks):
            for zh in range(repeat):
                dest = ((core_ref[0] ^ other) * blocks + b) * repeat + zh
                out_ref[dest] = ordered[:, b * cols : (b + 1) * cols]


def terms_kernel(blk, mask_ref, core_ref, amp_ref, other_amp_ref, ints_ref, out_ref, all_ref):
    step = pl.program_id(0)
    rows, cols = ints_ref.shape
    dests, some, lanes = out_ref.shape
    side, slab = 4, 8
    owners = some // slab
    half = side * some // 2
    some_rows = half // side
    part_cols = amp_ref.shape[1]

    @pl.when(step == 0)
    def _():
        for core, ref in [(core_ref[0], amp_ref), (core_ref[0] ^ 1, other_amp_ref)]:
            for y in range(side):
                at = pl.multiple_of(core * half + y * some_rows, some_rows)
                for z in range(rows // part_cols):
                    start = (y * (rows // part_cols) + z) * some_rows
                    all_ref[pl.ds(at, some_rows), z * part_cols : (z + 1) * part_cols] = ref[
                        start : start + some_rows, :
                    ]

    terms = []
    for col in range(cols // blk):
        total = None
        for row in range(rows // blk):
            keep = mask_ref[row, step * (cols // blk) + col].astype(F32)
            term = keep * mm(
                all_ref[:, row * blk : (row + 1) * blk],
                ints_ref[row * blk : (row + 1) * blk, col * blk : (col + 1) * blk],
            )
            total = term if total is None else total + term
        terms.append(total)
    terms = jnp.concatenate(terms, axis=1)
    for dest in range(dests):
        z, y = dest // side, dest % side
        cut = slice(z * lanes, (z + 1) * lanes)
        part = []
        for o in range(owners):
            at = o % 2 * half + y * some_rows + o // 2 * slab
            part.append(terms[at : at + slab, cut])
        out_ref[dest] = jnp.concatenate(part, axis=0).astype(BF16)


def sum_terms_kernel(nuw, owners, in_ref, out_ref):
    parts, rows, cols = in_ref.shape
    dests, lams, lanes = out_ref.shape
    some = rows // owners
    total = in_ref[0].astype(F32)
    for part in range(1, parts):
        total = total + in_ref[part].astype(F32)
    total = total.astype(BF16)
    wide_rows = owners * lanes
    row = row_ids(wide_rows)
    source = jnp.where(mod(row, lanes) < nuw * some, div(row, lanes) * some + mod(row, some), -1)
    wide = mm(ones_where(source == lane_ids(rows)), total)
    own = div(mod(row, lanes), some) == mod(lane_ids(cols), nuw)
    wide = jnp.where(own, wide, 0.0).astype(BF16)
    collect = ones_where(div(lane_ids(cols), nuw) == row_ids(lams))
    ordered = lax.dot_general(collect, wide, LANES, preferred_element_type=F32).astype(BF16)
    for dest in range(dests):
        o = dest // (dests // owners)
        out_ref[dest] = ordered[:, o * lanes : (o + 1) * lanes]


def forward_kernel(core_ref, in_ref, coef_ref, lad_ref, out_ref):
    dests, padded, lanes = out_ref.shape
    owners, lams, _ = lad_ref.shape
    mus = owners * lams // 2
    fwd = None
    for other in range(2):
        coef = coef_ref[...] if other else in_ref[:, :, :mus]
        start = (core_ref[0] ^ other) * (owners // 2)
        ladder = lad_ref[pl.ds(start, owners // 2)].reshape(mus, lanes)
        part = mm(coef.reshape(dests * padded, mus), ladder)
        fwd = part if fwd is None else fwd + part
    out_ref[...] = fwd.astype(BF16).reshape(out_ref.shape)


def out_kernel(few, fwd_ref, win_ref, out_ref, rows_ref):
    step = pl.program_id(0)
    parts, total, lanes = fwd_ref.shape
    nuw = win_ref.shape[0]
    virt, pairs, _ = out_ref.shape
    side = pairs // few
    rows = virt * pairs

    @pl.when(step == 0)
    def _():
        joined = []
        for y in range(side):
            fwd = None
            for low in range(parts // side):
                part = fwd_ref[y * (parts // side) + low].astype(F32)
                fwd = part if fwd is None else fwd + part
            joined.append(fwd)
        joined = jnp.concatenate(joined, axis=1).astype(BF16)
        every = rows_ref.shape[0]
        spread = ones_where(div(lane_ids(every), pairs) == row_ids(total))
        lane = row_ids(side * lanes)
        pair_of = div(lane, lanes) * few + mod(lane, few)
        pair_of = jnp.where(mod(lane, lanes) < nuw * few, pair_of, -1)
        wide = lax.dot_general(joined, spread, ROWS, preferred_element_type=F32)
        wide = jnp.where(pair_of == mod(lane_ids(every), pairs), wide, 0.0).astype(BF16)
        pick = ones_where(div(mod(lane_ids(side * lanes), lanes), few) == row_ids(rows_ref.shape[1]))
        rows_ref[...] = mm(pick, wide).T.astype(BF16)

    fwd = rows_ref[pl.ds(pl.multiple_of(step * rows, rows), rows), :]
    out_ref[...] = mm(fwd[:, :nuw], win_ref[...]).astype(BF16).reshape(out_ref.shape)


def params(mib=24):
    return pltpu.CompilerParams(vmem_limit_bytes=mib * 1024 * 1024)


def swap(array, axis):
    return lax.ppermute(array, axis, [(0, 1), (1, 0)])


def exchange(array, axes):
    return lax.all_to_all(array, axes, split_axis=0, concat_axis=0, tiled=True)


def local(sizes, amplitudes, window_coef, virtual_coef, integrals, block_mask):
    pairs, virt, _ = amplitudes.shape
    nuw, nv = window_coef.shape
    nao = virtual_coef.shape[0]
    rows, cols = integrals.shape
    side = sizes["y"]
    sp = side * sizes["z"] * sizes["x"]
    op = sizes["zh"] * sizes["core"]
    few = pairs // side
    mus = nao * side // sp
    width = 128
    steps = 4
    padded = -(-virt // 16) * 16
    amp = jnp.transpose(amplitudes, (1, 0, 2))
    coef = jnp.transpose(virtual_coef, (1, 0))
    my_core = lax.axis_index("core").reshape(1)
    smem = pl.BlockSpec(memory_space=pltpu.SMEM)
    hbm = pl.BlockSpec(memory_space=pltpu.HBM)
    vmem = pl.BlockSpec(memory_space=pltpu.VMEM)

    sent = pl.pallas_call(
        functools.partial(half_kernel, steps, few),
        in_specs=[smem, hbm, hbm, hbm],
        out_specs=vmem,
        out_shape=jax.ShapeDtypeStruct((sp, padded, mus // 2 + width), BF16),
        scratch_shapes=[
            pltpu.VMEM((virt, pairs, nv), BF16),
            pltpu.VMEM((nuw, nv), BF16),
            pltpu.VMEM((virt, nao // 2), BF16),
            pltpu.SemaphoreType.DMA((steps + 2,)),
        ],
        compiler_params=params(52),
        name="half",
    )(my_core, amp, window_coef, coef)
    chunk = exchange(sent, ("y", "z", "x"))
    other_coef = swap(chunk[:, :, : mus // 2], "core")
    some = nuw * mus * side // sp
    ao_amp = pl.pallas_call(
        functools.partial(amp_kernel, nuw),
        in_specs=[smem, vmem, vmem],
        out_specs=vmem,
        out_shape=jax.ShapeDtypeStruct((sp // sizes["x"] * sizes["zh"], few, some), BF16),
        compiler_params=params(),
        name="amp",
    )(my_core, chunk, other_coef)
    amp_here = exchange(ao_amp, ("y", "z", "zh")).reshape(-1, some)
    amp_there = swap(amp_here, "core")

    wide = cols // sizes["x"]
    part = wide // sizes["z"]
    whole = lambda array: pl.BlockSpec(array.shape, lambda i: (0, 0))
    terms = pl.pallas_call(
        functools.partial(terms_kernel, rows // block_mask.shape[0]),
        grid=(sizes["x"],),
        in_specs=[
            smem,
            smem,
            whole(amp_here),
            whole(amp_there),
            pl.BlockSpec((rows, wide), lambda i: (0, i)),
        ],
        out_specs=pl.BlockSpec((side * sizes["z"], op * few, part), lambda i: (i, 0, 0)),
        out_shape=jax.ShapeDtypeStruct((sp, op * few, part), BF16),
        scratch_shapes=[pltpu.VMEM((op * pairs, rows), BF16)],
        compiler_params=params(52),
        name="terms",
    )(block_mask, my_core, amp_here, amp_there, integrals)
    pieces = exchange(terms, ("x", "z", "y"))
    ladder = pl.pallas_call(
        functools.partial(sum_terms_kernel, nuw, op),
        out_shape=jax.ShapeDtypeStruct((op, part // nuw, width), BF16),
        compiler_params=params(),
        name="sum_terms",
    )(pieces)
    owned = exchange(ladder, ("zh", "core"))
    fwd = pl.pallas_call(
        forward_kernel,
        in_specs=[smem, vmem, vmem, vmem],
        out_specs=vmem,
        out_shape=jax.ShapeDtypeStruct((sp, padded, width), BF16),
        compiler_params=params(),
        name="forward",
    )(my_core, chunk, other_coef, owned)
    fwd = exchange(fwd, ("y", "z", "x"))
    out = pl.pallas_call(
        functools.partial(out_kernel, few),
        grid=(steps,),
        in_specs=[pl.BlockSpec(fwd.shape, lambda i: (0, 0, 0)), whole(window_coef)],
        out_specs=pl.BlockSpec((virt // steps, pairs, nv), lambda i: (i, 0, 0)),
        out_shape=jax.ShapeDtypeStruct((virt, pairs, nv), BF16),
        scratch_shapes=[pltpu.VMEM((virt * pairs, 16), BF16)],
        compiler_params=params(),
        name="out",
    )(fwd, window_coef)
    return jnp.transpose(out, (1, 0, 2))


def solution(mesh):
    sizes = {"y": 4, "z": 2, "x": 4, "zh": 4, "core": 2}
    fine = Mesh(mesh.devices.reshape(tuple(sizes.values())), tuple(sizes))
    sp, op = ("y", "z", "x"), ("zh", "core")
    placed = (P(op, sp, None), P(), P(None, sp), P(sp, op), P(sp, op))
    return jax.shard_map(
        functools.partial(local, sizes),
        mesh=fine,
        in_specs=placed,
        out_specs=P(op, sp, None),
        check_vma=False,
    )
```

time: 495 us -> 116 us (0.23)
  waiting for transfers between devices: 161 us -> 3.15 us
  blocking collectives: 238 us -> 95 us
  local copies, waits for them, and re-layouts: 59.8 us -> 1.79 us
  matrix products: 17.4 us -> 0 us
  Pallas kernels: 0 us -> 15.4 us
  between operations: 13.5 us -> 0.06 us
    psum x1 -> x0, blocking collectives: 183 us -> none  [local(): ladder = lax.psum(terms, 'sp').astype(jnp.bfloat16)]
    reduce_scatter x1 -> x0, waiting for transfers between devices: 161 us -> none  [local(): lax.psum_scatter(partial_amp, 'sp', scatter_dimension=1, tiled=True)]
    all_to_all x1 -> x5, blocking collectives: 38.3 us -> 95 us  [exchange(): return lax.all_to_all(array, axes, split_axis=0, concat_axis=0, tiled=True)]
    reshape x3 -> x0, local copies, waits for them, and re-layouts: 35.6 us -> none  [the longest x2 24 us: local(): partial_amp = partial_amp.reshape(own_pairs, NPAIR)]
    dot_general x5 -> x0, matrix products: 17.4 us -> none  [the longest x1 5.18 us: local(): terms = jnp.dot(all_amp, screened, preferred_element_type=jnp.float32)]
    all_gather x1 -> x0, blocking collectives: 16.6 us -> none  [local(): all_amp = lax.all_gather(ao_amp, 'op', axis=0, tiled=True)]
    pallas_call x0 -> x6, Pallas kernels: none -> 15.4 us  [the longest x1 4.89 us: local(): pl.pallas_call(functools.partial(half_kernel, steps, few), in_specs=[smem...]
    transpose x1 -> x0, local copies, waits for them, and re-layouts: 11.2 us -> none  [local(): jnp.einsum('ma,pan->pmn', virtual_coef, half, preferred_element_type=jnp....]
  transfers between devices with their start and end apart: 1 -> 2, of which waited for: 1 -> 2; matrix products, arithmetic and copies ran while one was open for 1% -> 0% of each run, Pallas kernels for 0% -> 0%
where the time goes in v1:
time: 116 us
  blocking collectives  95 us (82%)
  Pallas kernels  15.4 us (13%)
  waiting for transfers between devices  3.15 us (3%)
  local copies, waits for them, and re-layouts  1.79 us (2%)
    all_to_all x5, blocking collectives, exchange(): return lax.all_to_all(array, axes, split_axis=0, concat_axis=0, tiled=True)  95 us
    pallas_call x1, Pallas kernels, local(): pl.pallas_call(functools.partial(half_kernel, steps, few), in_specs=[smem...  4.89 us
    pallas_call x1, Pallas kernels, local(): pl.pallas_call(functools.partial(terms_kernel, rows // block_mask.shape[0...  4.19 us
    pallas_call x1, Pallas kernels, local(): pl.pallas_call(functools.partial(out_kernel, few), grid=(steps,), in_spec...  3.92 us
    ppermute x2, waiting for transfers between devices, swap(): return lax.ppermute(array, axis, [(0, 1), (1, 0)])  3.15 us
  transfers between devices with their start and end apart: 2, of which 2 were waited for; matrix products, arithmetic and copies ran while one was open for 0% of the time, Pallas kernels for 0%

profile of v1, /device:TPU:2, one launch (start us, length us, event | category | flops | bytes accessed | tf_op | source)
XLA Modules:
  0.0 115.5 jit_solution(5822511270740159511)
XLA Ops:
  0.0 0.0 copy-start
  0.0 0.9 copy-done
  0.9 0.0 copy-start.1
  0.9 0.8 copy-done.1
  1.7 0.0 copy-start.3
  1.7 4.9 %half.1 = bf16[32,48,256]{2,1,0:T(8,128)(2,1)S(1)} custom-call(s32[1]{0:T(128)} %bitcast.core_ref, bf16[44,32,1408]{2,1,0:T(8,128)(2,1)} %bitcast.8, bf16[12,1408]{1,0:T(8,128)(2,1)S(1)} %copy-done.1, bf16[44,2048]{1,0:T(8,128)(2,1)S(1)} %bitcast.7), custom_call_target="tpu_custom_call" | custom-call | tf_op jit(solution)/shard_map/half/pallas_call | solution.py:274
  6.6 22.3 %all_to_all.25.in_ref = bf16[32,48,256]{2,1,0:T(8,128)(2,1)S(1)} all-to-all(bf16[32,48,256]{2,1,0:T(8,128)(2,1)S(1)} %half.1), channel_id=1, replica_groups=mesh['y'=4,'z'=2,'x'=4,'zh'=4,'core'=2] {'y','z','x'}, dimensions={0} | all-to-all | bytes 1572864 | tf_op jit(solution)/shard_map/all_to_all | solution.py:251
  28.9 0.1 slice.4
  29.0 0.1 collective-permute-start
  29.1 1.7 %collective-permute-done.coef_ref = bf16[32,48,128]{2,1,0:T(8,128)(2,1)S(1)} collective-permute-done((bf16[32,48,128]{2,1,0:T(8,128)(2,1)S(1)}, bf16[32,48,128]{2,1,0:T(8,128)(2,1)S(1)}, u32[]{:S(2)}, u32[]{:S(2)}) %collective-permute-start) | collective-permute-done | bytes 393248 | tf_op jit(solution)/shard_map/ppermute | solution.py:247
  30.8 1.4 %amp.1 = bf16[32,8,384]{2,1,0:T(8,128)(2,1)S(1)} custom-call(s32[1]{0:T(128)} %bitcast.core_ref, bf16[32,48,256]{2,1,0:T(8,128)(2,1)S(1)} %all_to_all.25.in_ref, bf16[32,48,128]{2,1,0:T(8,128)(2,1)S(1)} %collective-permute-done.coef_ref), custom_call_target="tpu_custom_call" | custom-call | tf_op jit(solution)/shard_map/amp/pallas_call | solution.py:291
  32.1 19.3 %all_to_all.26 = bf16[32,8,384]{2,1,0:T(8,128)(2,1)S(1)} all-to-all(bf16[32,8,384]{2,1,0:T(8,128)(2,1)S(1)} %amp.1), channel_id=1, replica_groups=mesh['y'=4,'z'=2,'x'=4,'zh'=4,'core'=2] {'y','z','zh'}, dimensions={0} | all-to-all | bytes 393216 | tf_op jit(solution)/shard_map/all_to_all | solution.py:251
  51.4 0.0 collective-permute-start.1
  51.4 1.4 %collective-permute-done.1.other_amp_ref = bf16[256,384]{1,0:T(8,128)(2,1)S(1)} collective-permute-done((bf16[256,384]{1,0:T(8,128)(2,1)S(1)}, bf16[256,384]{1,0:T(8,128)(2,1)S(1)}, u32[]{:S(2)}, u32[]{:S(2)}) %collective-permute-start.1) | collective-permute-done | bytes 196640 | tf_op jit(solution)/shard_map/ppermute | solution.py:247
  52.9 0.0 copy-done.3
  52.9 4.2 %terms.1 = bf16[32,64,384]{2,1,0:T(8,128)(2,1)S(1)} custom-call(s32[3,12]{1,0:T(4,128)S(1)} %copy-done.3, s32[1]{0:T(128)} %bitcast.core_ref, bf16[256,384]{1,0:T(8,128)(2,1)S(1)} %bitcast.6, bf16[256,384]{1,0:T(8,128)(2,1)S(1)} %collective-permute-done.1.other_amp_ref, bf16[768,3072]{1,0:T(8,128)(2,1)} %ints_ref.1), custom_call_target="tpu_custom_call" | custom-call | tf_op jit(solution)/shard_map/terms/pallas_call | solution.py:305
  57.1 0.0 copy-start.2
  57.1 27.8 %all_to_all.27.in_ref = bf16[32,64,384]{2,1,0:T(8,128)(2,1)S(1)} all-to-all(bf16[32,64,384]{2,1,0:T(8,128)(2,1)S(1)} %terms.1), channel_id=1, replica_groups=mesh['y'=4,'z'=2,'x'=4,'zh'=4,'core'=2] {'x','z','y'}, dimensions={0} | all-to-all | bytes 3145728 | tf_op jit(solution)/shard_map/all_to_all | solution.py:251
  84.9 0.7 sum_terms.1
  85.7 11.2 %all_to_all.28.lad_ref = bf16[8,32,128]{2,1,0:T(8,128)(2,1)S(1)} all-to-all(bf16[8,32,128]{2,1,0:T(8,128)(2,1)S(1)} %sum_terms.1), channel_id=1, replica_groups=mesh['y'=4,'z'=2,'x'=4,'zh'=4,'core'=2] {'zh','core'}, dimensions={0} | all-to-all | bytes 131072 | tf_op jit(solution)/shard_map/all_to_all | solution.py:251
  96.8 0.3 forward.1
  97.2 14.4 %all_to_all.29.fwd_ref = bf16[32,48,128]{2,1,0:T(8,128)(2,1)S(1)} all-to-all(bf16[32,48,128]{2,1,0:T(8,128)(2,1)S(1)} %forward.1), channel_id=1, replica_groups=mesh['y'=4,'z'=2,'x'=4,'zh'=4,'core'=2] {'y','z','x'}, dimensions={0} | all-to-all | bytes 786432 | tf_op jit(solution)/shard_map/all_to_all | solution.py:251
  111.6 0.0 copy-done.2
  111.6 3.9 %out.1 = bf16[44,32,1408]{2,1,0:T(8,128)(2,1)} custom-call(bf16[32,48,128]{2,1,0:T(8,128)(2,1)S(1)} %all_to_all.29.fwd_ref, bf16[12,1408]{1,0:T(8,128)(2,1)S(1)} %copy-done.2), custom_call_target="tpu_custom_call" | custom-call | tf_op jit(solution)/shard_map/out/pallas_call | solution.py:338
Async XLA Ops:
  0.0 0.9 copy-start
  0.9 0.8 copy-start.1
  1.7 51.2 %copy-start.3 = (s32[3,12]{1,0:T(4,128)S(1)}, s32[3,12]{1,0:T(4,128)}, u32[]{:S(2)}) copy-start(s32[3,12]{1,0:T(4,128)} %mask_ref.1) | copy-start | bytes 436
  29.0 1.8 %collective-permute-start = (bf16[32,48,128]{2,1,0:T(8,128)(2,1)S(1)}, bf16[32,48,128]{2,1,0:T(8,128)(2,1)S(1)}, u32[]{:S(2)}, u32[]{:S(2)}) collective-permute-start(bf16[32,48,128]{2,1,0:T(8,128)(2,1)S(1)} %slice.4), channel_id=1, source_target_pairs={{0,1},{1,0},{2,3},{3,2},{4,5},{5,4},{6,7},{7,6},{8,9},{9,8},{10,11... | collective-permute-start | bytes 1179656 | tf_op jit(solution)/shard_map/ppermute | solution.py:247
  51.4 1.4 %collective-permute-start.1 = (bf16[256,384]{1,0:T(8,128)(2,1)S(1)}, bf16[256,384]{1,0:T(8,128)(2,1)S(1)}, u32[]{:S(2)}, u32[]{:S(2)}) collective-permute-start(bf16[256,384]{1,0:T(8,128)(2,1)S(1)} %bitcast.5), channel_id=1, source_target_pairs={{0,1},{1,0},{2,3},{3,2},{4,5},{5,4},{6,7},{7,6},{8,9},{9,8},{10,11... | collective-permute-start | bytes 589832 | tf_op jit(solution)/shard_map/ppermute | solution.py:247
  57.1 54.5 %copy-start.2 = (bf16[12,1408]{1,0:T(8,128)(2,1)S(1)}, bf16[12,1408]{1,0:T(8,128)(2,1)}, u32[]{:S(2)}) copy-start(bf16[12,1408]{1,0:T(8,128)(2,1)} %win_ref.1) | copy-start | bytes 101380

commit v2 on v1

v2 whole, which is shorter than its diff:
```python
import functools

import jax
import jax.numpy as jnp
from jax import lax
from jax.experimental import pallas as pl
from jax.experimental.pallas import tpu as pltpu
from jax.sharding import Mesh
from jax.sharding import PartitionSpec as P

F32 = jnp.float32
BF16 = jnp.bfloat16
ROWS = (((0,), (0,)), ((), ()))
LANES = (((1,), (1,)), ((), ()))


def iota(shape, dim):
    return lax.broadcasted_iota(jnp.int32, shape, dim)


def div(x, n):
    if n & (n - 1) == 0:
        return lax.shift_right_logical(x, n.bit_length() - 1)
    return lax.shift_right_logical(x * ((1 << 19) // n + 1), 19)


def mod(x, n):
    return x & (n - 1) if n & (n - 1) == 0 else x - div(x, n) * n


def row_ids(size):
    return iota((size, 1), 0)


def lane_ids(size):
    return iota((1, size), 1)


def ones_where(cond):
    return jnp.where(cond, 1.0, 0.0).astype(BF16)


def mm(x, y):
    return jnp.dot(x, y, preferred_element_type=F32)


def repeated(win, few, width):
    nuw, nv = win.shape
    win = jnp.broadcast_to(win.astype(F32)[:, None, :], (nuw, few, nv)).reshape(nuw * few, nv)
    return jnp.concatenate([win, jnp.zeros((width - nuw * few, nv), F32)], axis=0).astype(BF16)


def half_kernel(
    steps, few, core_ref, amp_hbm, win_hbm, coef_hbm, out_ref, amp_ref, win_ref, coef_ref, half_ref, sems
):
    total, pairs, _ = amp_hbm.shape
    dests, padded, lanes = out_ref.shape
    blocks, _, mus = coef_ref.shape
    width = lanes - mus
    side = pairs // few
    virt = total // steps
    rows = virt * pairs
    ahead = 3
    copies = [
        pltpu.make_async_copy(
            amp_hbm.at[step * virt : (step + 1) * virt],
            amp_ref.at[step * virt : (step + 1) * virt],
            sems.at[step],
        )
        for step in range(steps)
    ]
    win_copy = pltpu.make_async_copy(win_hbm, win_ref, sems.at[steps])
    coef_copies = []
    for b in range(blocks):
        start = pl.multiple_of((2 * b + core_ref[0]) * mus, mus)
        coef_copies.append(
            pltpu.make_async_copy(coef_hbm.at[:, pl.ds(start, mus)], coef_ref.at[b], sems.at[steps + 1 + b])
        )
    win_copy.start()
    for copy in copies[:ahead]:
        copy.start()
    for copy in coef_copies:
        copy.start()
    win_copy.wait()
    win = repeated(win_ref[...], few, width)
    own = mod(row_ids(few), few) == mod(lane_ids(width), few)
    out_ref[:, total:, :mus] = jnp.zeros((dests, padded - total, mus), BF16)
    for step in range(steps):
        copies[step].wait()
        if step + ahead < steps:
            copies[step + ahead].start()
        block = amp_ref[step * virt : (step + 1) * virt].reshape(rows, amp_ref.shape[2])
        deep = 768
        half = lax.dot_general(block[:, :deep], win[:, :deep], LANES, preferred_element_type=F32)
        half += lax.dot_general(block[:, deep:], win[:, deep:], LANES, preferred_element_type=F32)
        half = half.astype(BF16).astype(F32).reshape(virt, side, few, width)
        for x in range(side):
            part = jnp.sum(jnp.where(own, half[:, x], 0.0), axis=1)
            half_ref[x, step * virt : (step + 1) * virt, :] = part
        if step == 0:
            for b in range(blocks):
                coef_copies[b].wait()
                for x in range(side):
                    out_ref[b * side + x, :total, :mus] = coef_ref[b]
    half_ref[:, total:, :] = jnp.zeros((side, padded - total, width), F32)
    for x in range(side):
        half = half_ref[x].astype(BF16)
        for b in range(blocks):
            out_ref[b * side + x, :, mus:] = half


def amp_of(nuw, few, half, coef):
    depth, mus = coef.shape
    every = mus * nuw
    width = half.shape[1]
    amp = lax.dot_general(coef, half, ROWS, preferred_element_type=F32).astype(BF16)
    wide = mm(ones_where(div(row_ids(every), nuw) == lane_ids(mus)), amp)
    own = mod(row_ids(every), nuw) == div(lane_ids(width), few)
    wide = jnp.where(own, wide, 0.0).astype(BF16)
    pick = ones_where(row_ids(2 * few) == mod(lane_ids(width), few))
    return lax.dot_general(pick, wide, LANES, preferred_element_type=F32)[:few].astype(BF16)


def own_amp_kernel(nuw, in_ref, out_ref):
    parts, padded, lanes = in_ref.shape
    mus = lanes // 2
    coef = in_ref[:, :, :mus].reshape(parts * padded, mus)
    half = in_ref[:, :, mus:].reshape(parts * padded, mus)
    out_ref[...] = amp_of(nuw, out_ref.shape[0], half, coef)


def amp_kernel(nuw, core_ref, in_ref, coef_ref, own_ref, out_ref):
    parts, padded, lanes = in_ref.shape
    dests, few, cols = out_ref.shape
    mus = lanes // 2
    repeat = dests * cols // (2 * mus * nuw)
    blocks = dests // (2 * repeat)
    half = in_ref[:, :, mus:].reshape(parts * padded, mus)
    other_amp = amp_of(nuw, few, half, coef_ref[...].reshape(parts * padded, mus))
    for other, amp in enumerate([own_ref[...], other_amp]):
        for b in range(blocks):
            for zh in range(repeat):
                dest = ((core_ref[0] ^ other) * blocks + b) * repeat + zh
                out_ref[dest] = amp[:, b * cols : (b + 1) * cols]


def terms_kernel(blk, mask_ref, core_ref, amp_ref, other_amp_ref, ints_ref, out_ref, all_ref):
    step = pl.program_id(0)
    rows, cols = ints_ref.shape
    dests, few, _ = out_ref.shape
    half = amp_ref.shape[0]
    side = 4

    @pl.when(step == 0)
    def _():
        at = pl.multiple_of(core_ref[0] * half, half)
        all_ref[pl.ds(at, half), :] = amp_ref[...]
        at = pl.multiple_of((core_ref[0] ^ 1) * half, half)
        all_ref[pl.ds(at, half), :] = other_amp_ref[...]

    for col in range(cols // blk):
        total = None
        for row in range(rows // blk):
            keep = mask_ref[row, step * (cols // blk) + col].astype(F32)
            term = keep * mm(
                all_ref[:, row * blk : (row + 1) * blk],
                ints_ref[row * blk : (row + 1) * blk, col * blk : (col + 1) * blk],
            )
            total = term if total is None else total + term
        for dest in range(dests):
            o, x = dest // side, dest % side
            at = o % 2 * half + x * (half // side) + o // 2 * few
            out_ref[dest, :, col * blk : (col + 1) * blk] = total[at : at + few].astype(BF16)


def sum_terms_kernel(in_ref, out_ref):
    total = in_ref[0].astype(F32)
    for part in range(1, in_ref.shape[0]):
        total = total + in_ref[part].astype(F32)
    out_ref[...] = total.astype(BF16)


def forward_kernel(nuw, core_ref, in_ref, coef_ref, lad_ref, out_ref, order_ref):
    dests, padded, lanes = out_ref.shape
    few, cols = lad_ref.shape
    mus = cols // nuw // 2
    part_cols = 384
    run = part_cols // nuw
    row = row_ids(lanes)
    source = jnp.where(row < nuw * few, mod(row, few), -1)
    wide = mm(ones_where(source == lane_ids(few)), lad_ref[...])
    own = div(row, few) == mod(lane_ids(part_cols), nuw)
    collect = ones_where(div(lane_ids(part_cols), nuw) == row_ids(run))
    for part in range(cols // part_cols):
        some = wide[:, part * part_cols : (part + 1) * part_cols]
        some = jnp.where(own, some, 0.0).astype(BF16)
        some = lax.dot_general(collect, some, LANES, preferred_element_type=F32)
        order_ref[part * run : (part + 1) * run, :] = some.astype(BF16)
    fwd = None
    for other in range(2):
        coef = coef_ref[...] if other else in_ref[:, :, :mus]
        start = pl.multiple_of((core_ref[0] ^ other) * mus, mus)
        part = mm(coef.reshape(dests * padded, mus), order_ref[pl.ds(start, mus), :])
        fwd = part if fwd is None else fwd + part
    out_ref[...] = fwd.astype(BF16).reshape(out_ref.shape)


def out_kernel(steps, few, fwd_ref, win_ref, out_hbm, out_ref, sems):
    parts, _, lanes = fwd_ref.shape
    total, pairs, nv = out_ref.shape
    side = pairs // few
    virt = total // steps
    win = repeated(win_ref[...], few, lanes)
    own = row_ids(few) == mod(lane_ids(lanes), few)
    fwds = []
    for x in range(side):
        fwd = None
        for block in range(parts // side):
            part = fwd_ref[block * side + x].astype(F32)
            fwd = part if fwd is None else fwd + part
        fwds.append(fwd)
    copies = []
    for step in range(steps):
        cut = slice(step * virt, (step + 1) * virt)
        wide = [jnp.broadcast_to(fwd[cut][:, None, :], (virt, few, lanes)) for fwd in fwds]
        wide = jnp.concatenate([jnp.where(own, part, 0.0) for part in wide], axis=1)
        wide = wide.reshape(virt * pairs, lanes).astype(BF16)
        out_ref[cut] = mm(wide, win).astype(BF16).reshape(virt, pairs, nv)
        copies.append(pltpu.make_async_copy(out_ref.at[cut], out_hbm.at[cut], sems.at[step]))
        copies[-1].start()
    for copy in copies:
        copy.wait()


def params(mib=24):
    return pltpu.CompilerParams(vmem_limit_bytes=mib * 1024 * 1024)


def swap(array, axis):
    return lax.ppermute(array, axis, [(0, 1), (1, 0)])


def turn(array, sizes):
    square = sizes["y"] * sizes["z"]
    pairs = [(one, one % square * square + one // square) for one in range(square * square)]
    return lax.ppermute(array, ("y", "z", "zh", "core"), pairs)


def exchange(array, axes):
    return lax.all_to_all(array, axes, split_axis=0, concat_axis=0, tiled=True)


def local(sizes, amplitudes, window_coef, virtual_coef, integrals, block_mask):
    pairs, virt, _ = amplitudes.shape
    nuw, nv = window_coef.shape
    nao = virtual_coef.shape[0]
    rows, cols = integrals.shape
    side = sizes["y"]
    sp = side * sizes["z"] * sizes["x"]
    op = sizes["zh"] * sizes["core"]
    few = pairs // side
    mus = nao * side // sp
    width = 128
    steps = 4
    padded = -(-virt // 16) * 16
    amp = jnp.transpose(amplitudes, (1, 0, 2))
    coef = jnp.transpose(virtual_coef, (1, 0))
    my_core = lax.axis_index("core").reshape(1)
    smem = pl.BlockSpec(memory_space=pltpu.SMEM)
    hbm = pl.BlockSpec(memory_space=pltpu.HBM)
    vmem = pl.BlockSpec(memory_space=pltpu.VMEM)

    sent = pl.pallas_call(
        functools.partial(half_kernel, steps, few),
        in_specs=[smem, hbm, hbm, hbm],
        out_specs=vmem,
        out_shape=jax.ShapeDtypeStruct((sp, padded, mus // 2 + width), BF16),
        scratch_shapes=[
            pltpu.VMEM((virt, pairs, nv), BF16),
            pltpu.VMEM((nuw, nv), BF16),
            pltpu.VMEM((nao // mus, virt, mus // 2), BF16),
            pltpu.VMEM((side, padded, width), F32),
            pltpu.SemaphoreType.DMA((steps + 1 + nao // mus,)),
        ],
        compiler_params=params(54),
        name="half",
    )(my_core, amp, window_coef, coef)
    chunk = exchange(sent, ("y", "z", "x"))
    other_coef = swap(chunk[:, :, : mus // 2], "core")
    flat = sizes["x"] * sizes["zh"]
    own_amp = pl.pallas_call(
        functools.partial(own_amp_kernel, nuw),
        out_shape=jax.ShapeDtypeStruct((few, mus // 2 * nuw), BF16),
        compiler_params=params(),
        name="own_amp",
    )(chunk)
    ao_amp = pl.pallas_call(
        functools.partial(amp_kernel, nuw),
        in_specs=[smem, vmem, vmem, vmem],
        out_specs=vmem,
        out_shape=jax.ShapeDtypeStruct((flat, few, rows), BF16),
        compiler_params=params(),
        name="amp",
    )(my_core, chunk, other_coef, own_amp)
    amp_here = exchange(ao_amp, ("x", "zh")).reshape(flat * few, rows)
    amp_there = swap(amp_here, "core")

    wide = cols // 4
    whole = lambda array: pl.BlockSpec(array.shape, lambda i: (0, 0))
    terms = pl.pallas_call(
        functools.partial(terms_kernel, rows // block_mask.shape[0]),
        grid=(cols // wide,),
        in_specs=[
            smem,
            smem,
            whole(amp_here),
            whole(amp_there),
            pl.BlockSpec((rows, wide), lambda i: (0, i)),
        ],
        out_specs=pl.BlockSpec((sp, few, wide), lambda i: (0, 0, i)),
        out_shape=jax.ShapeDtypeStruct((sp, few, cols), BF16),
        scratch_shapes=[pltpu.VMEM((op * pairs, rows), BF16)],
        compiler_params=params(24),
        name="terms",
    )(block_mask, my_core, amp_here, amp_there, integrals)
    pieces = exchange(terms, ("y", "z", "x"))
    ladder = pl.pallas_call(
        sum_terms_kernel,
        out_shape=jax.ShapeDtypeStruct((few, cols), BF16),
        compiler_params=params(),
        name="sum_terms",
    )(pieces)
    owned = turn(ladder, sizes)
    fwd = pl.pallas_call(
        functools.partial(forward_kernel, nuw),
        in_specs=[smem, vmem, vmem, vmem],
        out_specs=vmem,
        out_shape=jax.ShapeDtypeStruct((sp, padded, width), BF16),
        scratch_shapes=[pltpu.VMEM((mus, width), BF16)],
        compiler_params=params(),
        name="forward",
    )(my_core, chunk, other_coef, owned)
    fwd = exchange(fwd, ("y", "z", "x"))
    out = pl.pallas_call(
        functools.partial(out_kernel, steps, few),
        in_specs=[vmem, vmem],
        out_specs=hbm,
        out_shape=jax.ShapeDtypeStruct((virt, pairs, nv), BF16),
        scratch_shapes=[pltpu.VMEM((virt, pairs, nv), BF16), pltpu.SemaphoreType.DMA((steps,))],
        compiler_params=params(),
        name="out",
    )(fwd, window_coef)
    return jnp.transpose(out, (1, 0, 2))


def solution(mesh):
    sizes = {"y": 4, "z": 2, "x": 4, "zh": 4, "core": 2}
    fine = Mesh(mesh.devices.reshape(tuple(sizes.values())), tuple(sizes))
    sp, op = ("y", "z", "x"), ("zh", "core")
    placed = (P(op, sp, None), P(), P(None, sp), P(sp, op), P(sp, op))
    return jax.shard_map(
        functools.partial(local, sizes),
        mesh=fine,
        in_specs=placed,
        out_specs=P(op, sp, None),
        check_vma=False,
    )
```

time: 116 us -> 112 us (0.966)
  Pallas kernels: 15.4 us -> 13.2 us
  local copies, waits for them, and re-layouts: 1.79 us -> 0.09 us
    unnamed x8, local copies, waits for them, and re-layouts: 1.72 us -> 0.02 us
    pallas_call x1, Pallas kernels: 4.19 us -> 2.95 us  [local(): pl.pallas_call(functools.partial(terms_kernel, rows // block_mask.shape[0...]
    pallas_call x3 -> x4, Pallas kernels: 4.98 us -> 4.33 us  [the longest x1 2.41 us: local(): pl.pallas_call(functools.partial(out_kernel, steps, few), in_specs=[vmem,...]
    all_to_all x5 -> x4, blocking collectives: 95 us -> 94.9 us  [exchange(): return lax.all_to_all(array, axes, split_axis=0, concat_axis=0, tiled=True)]
  transfers between devices with their start and end apart: 2 -> 3, of which waited for: 2 -> 2; matrix products, arithmetic and copies ran while one was open for 0% -> 0% of each run, Pallas kernels for 0% -> 1%
where the time goes in v2:
time: 112 us; the launch traced here: 111 us
  blocking collectives  94.9 us (85%)
  Pallas kernels  13.2 us (12%)
  waiting for transfers between devices  2.39 us (2%)
    all_to_all x4, blocking collectives, exchange(): return lax.all_to_all(array, axes, split_axis=0, concat_axis=0, tiled=True)  94.9 us
    pallas_call x1, Pallas kernels, local(): pl.pallas_call(functools.partial(half_kernel, steps, few), in_specs=[smem...  5.12 us
    pallas_call x1, Pallas kernels, local(): pl.pallas_call(functools.partial(terms_kernel, rows // block_mask.shape[0...  2.95 us
    pallas_call x1, Pallas kernels, local(): pl.pallas_call(functools.partial(out_kernel, steps, few), in_specs=[vmem,...  2.41 us
    ppermute x2, waiting for transfers between devices, swap(): return lax.ppermute(array, axis, [(0, 1), (1, 0)])  2.38 us
  transfers between devices with their start and end apart: 3, of which 2 were waited for; matrix products, arithmetic and copies ran while one was open for 0% of the time, Pallas kernels for 1%

profile of v2, /device:TPU:2, one launch (start us, length us, event | category | flops | bytes accessed | tf_op | source)
XLA Modules:
  0.0 111.4 jit_solution(4243464733404689676)
XLA Ops:
  0.0 0.0 slice-start
  0.0 0.0 slice-start.1
  0.0 0.0 copy-start.1
  0.0 5.1 %half.1 = bf16[32,48,256]{2,1,0:T(8,128)(2,1)} custom-call(s32[1]{0:T(128)} %bitcast.core_ref, bf16[44,32,1408]{2,1,0:T(8,128)(2,1)} %bitcast.9, bf16[12,1408]{1,0:T(8,128)(2,1)} %win_ref.1, bf16[44,2048]{1,0:T(8,128)(2,1)} %bitcast.10), custom_call_target="tpu_custom_call" | custom-call | tf_op jit(solution)/shard_map/half/pallas_call | solution.py:273
  5.1 22.5 %all_to_all.20.in_ref = bf16[32,48,256]{2,1,0:T(8,128)(2,1)S(1)} all-to-all(bf16[32,48,256]{2,1,0:T(8,128)(2,1)} %half.1), channel_id=1, replica_groups=mesh['y'=4,'z'=2,'x'=4,'zh'=4,'core'=2] {'y','z','x'}, dimensions={0} | all-to-all | bytes 1572864 | tf_op jit(solution)/shard_map/all_to_all | solution.py:250
  27.6 0.1 slice.4
  27.7 0.1 collective-permute-start
  27.8 0.8 own_amp.1.own_ref
  28.6 0.9 collective-permute-done.coef_ref
  29.5 0.8 amp.1
  30.3 19.4 %all_to_all.21 = bf16[16,8,768]{2,1,0:T(8,128)(2,1)S(1)} all-to-all(bf16[16,8,768]{2,1,0:T(8,128)(2,1)S(1)} %amp.1), channel_id=1, replica_groups=mesh['y'=4,'z'=2,'x'=4,'zh'=4,'core'=2] {'x','zh'}, dimensions={0} | all-to-all | bytes 393216 | tf_op jit(solution)/shard_map/all_to_all | solution.py:250
  49.7 0.0 collective-permute-start.1
  49.7 1.4 %collective-permute-done.1.other_amp_ref = bf16[128,768]{1,0:T(8,128)(2,1)S(1)} collective-permute-done((bf16[128,768]{1,0:T(8,128)(2,1)S(1)}, bf16[128,768]{1,0:T(8,128)(2,1)S(1)}, u32[]{:S(2)}, u32[]{:S(2)}) %collective-permute-start.1) | collective-permute-done | bytes 196640 | tf_op jit(solution)/shard_map/ppermute | solution.py:240
  51.2 0.0 slice-done
  51.2 0.0 slice-done.1
  51.2 0.0 copy-done.1
  51.2 3.0 %terms.1 = bf16[32,8,3072]{2,1,0:T(8,128)(2,1)S(1)} custom-call(s32[3,12]{1,0:T(4,128)S(1)} %copy-done.1, s32[1]{0:T(128)} %bitcast.core_ref, bf16[128,768]{1,0:T(8,128)(2,1)S(1)} %bitcast.8, bf16[128,768]{1,0:T(8,128)(2,1)S(1)} %collective-permute-done.1.other_amp_ref, bf16[768,3072]{1,0:T(8,128)(2,1)S(1)} %bitcast.6), custom_call_target="tpu_custom_call" | custom-call | tf_op jit(solution)/shard_map/terms/pallas_call | solution.py:310
  54.1 0.0 copy-start
  54.1 28.2 %all_to_all.22.in_ref = bf16[32,8,3072]{2,1,0:T(8,128)(2,1)S(1)} all-to-all(bf16[32,8,3072]{2,1,0:T(8,128)(2,1)S(1)} %terms.1), channel_id=1, replica_groups=mesh['y'=4,'z'=2,'x'=4,'zh'=4,'core'=2] {'y','z','x'}, dimensions={0} | all-to-all | bytes 3145728 | tf_op jit(solution)/shard_map/all_to_all | solution.py:250
  82.3 0.2 sum_terms.1
  82.6 0.7 collective-permute-start.2
  83.2 0.0 collective-permute-done.2.lad_ref
  83.2 0.9 forward.1
  84.2 24.8 %all_to_all.23.fwd_ref = bf16[32,48,128]{2,1,0:T(8,128)(2,1)S(1)} all-to-all(bf16[32,48,128]{2,1,0:T(8,128)(2,1)S(1)} %forward.1), channel_id=1, replica_groups=mesh['y'=4,'z'=2,'x'=4,'zh'=4,'core'=2] {'y','z','x'}, dimensions={0} | all-to-all | bytes 786432 | tf_op jit(solution)/shard_map/all_to_all | solution.py:250
  109.0 0.0 copy-done
  109.0 2.4 %out.1 = bf16[44,32,1408]{2,1,0:T(8,128)(2,1)} custom-call(bf16[32,48,128]{2,1,0:T(8,128)(2,1)S(1)} %all_to_all.23.fwd_ref, bf16[12,1408]{1,0:T(8,128)(2,1)S(1)} %copy-done), custom_call_target="tpu_custom_call" | custom-call | tf_op jit(solution)/shard_map/out/pallas_call | solution.py:344
  (1 shorter events, 0.0 us)
Async XLA Ops:
  0.0 51.2 %slice-start = ((s8[4718592]{0:T(1024)(128)(4,1)}), s8[4194304]{0:T(1024)(128)(4,1)S(1)}, s32[]{:S(2)}) async-start(s8[4718592]{0:T(1024)(128)(4,1)} %bitcast.5), calls=%async_computation.4 | async-start | bytes 8388608
  0.0 51.2 %slice-start.1 = ((s8[4718592]{0:T(1024)(128)(4,1)}), s8[524288]{0:T(1024)(128)(4,1)S(1)}, s32[]{:S(2)}) async-start(s8[4718592]{0:T(1024)(128)(4,1)} %bitcast.5), calls=%async_computation.5 | async-start | bytes 1048576
  0.0 51.2 %copy-start.1 = (s32[3,12]{1,0:T(4,128)S(1)}, s32[3,12]{1,0:T(4,128)}, u32[]{:S(2)}) copy-start(s32[3,12]{1,0:T(4,128)} %mask_ref.1) | copy-start | bytes 436
  27.7 1.8 %collective-permute-start = (bf16[32,48,128]{2,1,0:T(8,128)(2,1)S(1)}, bf16[32,48,128]{2,1,0:T(8,128)(2,1)S(1)}, u32[]{:S(2)}, u32[]{:S(2)}) collective-permute-start(bf16[32,48,128]{2,1,0:T(8,128)(2,1)S(1)} %slice.4), channel_id=1, source_target_pairs={{0,1},{1,0},{2,3},{3,2},{4,5},{5,4},{6,7},{7,6},{8,9},{9,8},{10,11... | collective-permute-start | bytes 1179656 | tf_op jit(solution)/shard_map/ppermute | solution.py:240
  49.7 1.4 %collective-permute-start.1 = (bf16[128,768]{1,0:T(8,128)(2,1)S(1)}, bf16[128,768]{1,0:T(8,128)(2,1)S(1)}, u32[]{:S(2)}, u32[]{:S(2)}) collective-permute-start(bf16[128,768]{1,0:T(8,128)(2,1)S(1)} %bitcast.7), channel_id=1, source_target_pairs={{0,1},{1,0},{2,3},{3,2},{4,5},{5,4},{6,7},{7,6},{8,9},{9,8},{10,11... | collective-permute-start | bytes 589832 | tf_op jit(solution)/shard_map/ppermute | solution.py:240
  54.1 54.9 %copy-start = (bf16[12,1408]{1,0:T(8,128)(2,1)S(1)}, bf16[12,1408]{1,0:T(8,128)(2,1)}, u32[]{:S(2)}) copy-start(bf16[12,1408]{1,0:T(8,128)(2,1)} %win_ref.1) | copy-start | bytes 101380
  82.6 0.7 collective-permute-start.2

commit v3 on v2

--- a/solution.py
+++ b/solution.py
@@ -60,7 +60,7 @@
     side = pairs // few
     virt = total // steps
     rows = virt * pairs
-    ahead = 3
+    ahead = 5
     copies = [
         pltpu.make_async_copy(
             amp_hbm.at[step * virt : (step + 1) * virt],
@@ -82,7 +82,8 @@
     for copy in coef_copies:
         copy.start()
     win_copy.wait()
-    win = repeated(win_ref[...], few, width)
+    spread = ones_where(div(lane_ids(width), few) == row_ids(win_ref.shape[0]))
+    win = lax.dot_general(win_ref[...], spread, ROWS, preferred_element_type=F32).astype(BF16)
     own = mod(row_ids(few), few) == mod(lane_ids(width), few)
     out_ref[:, total:, :mus] = jnp.zeros((dests, padded - total, mus), BF16)
     for step in range(steps):
@@ -90,9 +91,7 @@
         if step + ahead < steps:
             copies[step + ahead].start()
         block = amp_ref[step * virt : (step + 1) * virt].reshape(rows, amp_ref.shape[2])
-        deep = 768
-        half = lax.dot_general(block[:, :deep], win[:, :deep], LANES, preferred_element_type=F32)
-        half += lax.dot_general(block[:, deep:], win[:, deep:], LANES, preferred_element_type=F32)
+        half = mm(block, win)
         half = half.astype(BF16).astype(F32).reshape(virt, side, few, width)
         for x in range(side):
             part = jnp.sum(jnp.where(own, half[:, x], 0.0), axis=1)
@@ -159,14 +158,12 @@
         all_ref[pl.ds(at, half), :] = other_amp_ref[...]
 
     for col in range(cols // blk):
-        total = None
+        kept = []
         for row in range(rows // blk):
-            keep = mask_ref[row, step * (cols // blk) + col].astype(F32)
-            term = keep * mm(
-                all_ref[:, row * blk : (row + 1) * blk],
-                ints_ref[row * blk : (row + 1) * blk, col * blk : (col + 1) * blk],
-            )
-            total = term if total is None else total + term
+            keep = mask_ref[row, step * (cols // blk) + col].astype(F32).astype(BF16)
+            kept.append(all_ref[:, row * blk : (row + 1) * blk] * keep)
+        kept = jnp.concatenate(kept, axis=1)
+        total = mm(kept, ints_ref[:, col * blk : (col + 1) * blk])
         for dest in range(dests):
             o, x = dest // side, dest % side
             at = o % 2 * half + x * (half // side) + o // 2 * few
@@ -261,7 +258,7 @@
     few = pairs // side
     mus = nao * side // sp
     width = 128
-    steps = 4
+    steps, chunks = 4, 11
     padded = -(-virt // 16) * 16
     amp = jnp.transpose(amplitudes, (1, 0, 2))
     coef = jnp.transpose(virtual_coef, (1, 0))
@@ -271,7 +268,7 @@
     vmem = pl.BlockSpec(memory_space=pltpu.VMEM)
 
     sent = pl.pallas_call(
-        functools.partial(half_kernel, steps, few),
+        functools.partial(half_kernel, chunks, few),
         in_specs=[smem, hbm, hbm, hbm],
         out_specs=vmem,
         out_shape=jax.ShapeDtypeStruct((sp, padded, mus // 2 + width), BF16),
@@ -280,7 +277,7 @@
             pltpu.VMEM((nuw, nv), BF16),
             pltpu.VMEM((nao // mus, virt, mus // 2), BF16),
             pltpu.VMEM((side, padded, width), F32),
-            pltpu.SemaphoreType.DMA((steps + 1 + nao // mus,)),
+            pltpu.SemaphoreType.DMA((chunks + 1 + nao // mus,)),
         ],
         compiler_params=params(54),
         name="half",

time: 112 us -> 112 us (level)
  no operation moved by 1% of the time
where the time goes in v3:
time: 112 us
  blocking collectives  94.9 us (85%)
  Pallas kernels  13.7 us (12%)
  waiting for transfers between devices  2.38 us (2%)
    all_to_all x4, blocking collectives, exchange(): return lax.all_to_all(array, axes, split_axis=0, concat_axis=0, tiled=True)  94.9 us
    pallas_call x1, Pallas kernels, local(): pl.pallas_call(functools.partial(half_kernel, chunks, few), in_specs=[sme...  5.66 us
    pallas_call x1, Pallas kernels, local(): pl.pallas_call(functools.partial(terms_kernel, rows // block_mask.shape[0...  2.94 us
    pallas_call x1, Pallas kernels, local(): pl.pallas_call(functools.partial(out_kernel, steps, few), in_specs=[vmem,...  2.41 us
    ppermute x2, waiting for transfers between devices, swap(): return lax.ppermute(array, axis, [(0, 1), (1, 0)])  2.38 us
  transfers between devices with their start and end apart: 3, of which 2 were waited for; matrix products, arithmetic and copies ran while one was open for 0% of the time, Pallas kernels for 1%

profile of v3, /device:TPU:2, one launch (start us, length us, event | category | flops | bytes accessed | tf_op | source)
XLA Modules:
  0.0 111.9 jit_solution(16748125767892160320)
XLA Ops:
  0.0 0.0 slice-start
  0.0 0.0 slice-start.1
  0.0 0.0 copy-start.1
  0.0 5.7 %half.1 = bf16[32,48,256]{2,1,0:T(8,128)(2,1)} custom-call(s32[1]{0:T(128)} %bitcast.core_ref, bf16[44,32,1408]{2,1,0:T(8,128)(2,1)} %bitcast.9, bf16[12,1408]{1,0:T(8,128)(2,1)} %win_ref.1, bf16[44,2048]{1,0:T(8,128)(2,1)} %bitcast.10), custom_call_target="tpu_custom_call" | custom-call | tf_op jit(solution)/shard_map/half/pallas_call | solution.py:270
  5.7 22.5 %all_to_all.20.in_ref = bf16[32,48,256]{2,1,0:T(8,128)(2,1)S(1)} all-to-all(bf16[32,48,256]{2,1,0:T(8,128)(2,1)} %half.1), channel_id=1, replica_groups=mesh['y'=4,'z'=2,'x'=4,'zh'=4,'core'=2] {'y','z','x'}, dimensions={0} | all-to-all | bytes 1572864 | tf_op jit(solution)/shard_map/all_to_all | solution.py:247
  28.2 0.1 slice.4
  28.2 0.1 collective-permute-start
  28.3 0.8 own_amp.1.own_ref
  29.1 0.9 collective-permute-done.coef_ref
  30.0 0.8 amp.1
  30.8 19.4 %all_to_all.21 = bf16[16,8,768]{2,1,0:T(8,128)(2,1)S(1)} all-to-all(bf16[16,8,768]{2,1,0:T(8,128)(2,1)S(1)} %amp.1), channel_id=1, replica_groups=mesh['y'=4,'z'=2,'x'=4,'zh'=4,'core'=2] {'x','zh'}, dimensions={0} | all-to-all | bytes 393216 | tf_op jit(solution)/shard_map/all_to_all | solution.py:247
  50.3 0.0 collective-permute-start.1
  50.3 1.4 %collective-permute-done.1.other_amp_ref = bf16[128,768]{1,0:T(8,128)(2,1)S(1)} collective-permute-done((bf16[128,768]{1,0:T(8,128)(2,1)S(1)}, bf16[128,768]{1,0:T(8,128)(2,1)S(1)}, u32[]{:S(2)}, u32[]{:S(2)}) %collective-permute-start.1) | collective-permute-done | bytes 196640 | tf_op jit(solution)/shard_map/ppermute | solution.py:237
  51.7 0.0 slice-done
  51.7 0.0 slice-done.1
  51.7 0.0 copy-done.1
  51.7 2.9 %terms.1 = bf16[32,8,3072]{2,1,0:T(8,128)(2,1)S(1)} custom-call(s32[3,12]{1,0:T(4,128)S(1)} %copy-done.1, s32[1]{0:T(128)} %bitcast.core_ref, bf16[128,768]{1,0:T(8,128)(2,1)S(1)} %bitcast.8, bf16[128,768]{1,0:T(8,128)(2,1)S(1)} %collective-permute-done.1.other_amp_ref, bf16[768,3072]{1,0:T(8,128)(2,1)S(1)} %bitcast.6), custom_call_target="tpu_custom_call" | custom-call | tf_op jit(solution)/shard_map/terms/pallas_call | solution.py:307
  54.7 0.0 copy-start
  54.7 28.2 %all_to_all.22.in_ref = bf16[32,8,3072]{2,1,0:T(8,128)(2,1)S(1)} all-to-all(bf16[32,8,3072]{2,1,0:T(8,128)(2,1)S(1)} %terms.1), channel_id=1, replica_groups=mesh['y'=4,'z'=2,'x'=4,'zh'=4,'core'=2] {'y','z','x'}, dimensions={0} | all-to-all | bytes 3145728 | tf_op jit(solution)/shard_map/all_to_all | solution.py:247
  82.9 0.2 sum_terms.1
  83.1 0.7 collective-permute-start.2
  83.8 0.0 collective-permute-done.2.lad_ref
  83.8 0.9 forward.1
  84.7 24.8 %all_to_all.23.fwd_ref = bf16[32,48,128]{2,1,0:T(8,128)(2,1)S(1)} all-to-all(bf16[32,48,128]{2,1,0:T(8,128)(2,1)S(1)} %forward.1), channel_id=1, replica_groups=mesh['y'=4,'z'=2,'x'=4,'zh'=4,'core'=2] {'y','z','x'}, dimensions={0} | all-to-all | bytes 786432 | tf_op jit(solution)/shard_map/all_to_all | solution.py:247
  109.5 0.0 copy-done
  109.5 2.4 %out.1 = bf16[44,32,1408]{2,1,0:T(8,128)(2,1)} custom-call(bf16[32,48,128]{2,1,0:T(8,128)(2,1)S(1)} %all_to_all.23.fwd_ref, bf16[12,1408]{1,0:T(8,128)(2,1)S(1)} %copy-done), custom_call_target="tpu_custom_call" | custom-call | tf_op jit(solution)/shard_map/out/pallas_call | solution.py:341
  (1 shorter events, 0.0 us)
Async XLA Ops:
  0.0 51.7 %slice-start = ((s8[4718592]{0:T(1024)(128)(4,1)}), s8[4194304]{0:T(1024)(128)(4,1)S(1)}, s32[]{:S(2)}) async-start(s8[4718592]{0:T(1024)(128)(4,1)} %bitcast.5), calls=%async_computation.4 | async-start | bytes 8388608
  0.0 51.7 %slice-start.1 = ((s8[4718592]{0:T(1024)(128)(4,1)}), s8[524288]{0:T(1024)(128)(4,1)S(1)}, s32[]{:S(2)}) async-start(s8[4718592]{0:T(1024)(128)(4,1)} %bitcast.5), calls=%async_computation.5 | async-start | bytes 1048576
  0.0 51.7 %copy-start.1 = (s32[3,12]{1,0:T(4,128)S(1)}, s32[3,12]{1,0:T(4,128)}, u32[]{:S(2)}) copy-start(s32[3,12]{1,0:T(4,128)} %mask_ref.1) | copy-start | bytes 436
  28.2 1.8 %collective-permute-start = (bf16[32,48,128]{2,1,0:T(8,128)(2,1)S(1)}, bf16[32,48,128]{2,1,0:T(8,128)(2,1)S(1)}, u32[]{:S(2)}, u32[]{:S(2)}) collective-permute-start(bf16[32,48,128]{2,1,0:T(8,128)(2,1)S(1)} %slice.4), channel_id=1, source_target_pairs={{0,1},{1,0},{2,3},{3,2},{4,5},{5,4},{6,7},{7,6},{8,9},{9,8},{10,11... | collective-permute-start | bytes 1179656 | tf_op jit(solution)/shard_map/ppermute | solution.py:237
  50.3 1.4 %collective-permute-start.1 = (bf16[128,768]{1,0:T(8,128)(2,1)S(1)}, bf16[128,768]{1,0:T(8,128)(2,1)S(1)}, u32[]{:S(2)}, u32[]{:S(2)}) collective-permute-start(bf16[128,768]{1,0:T(8,128)(2,1)S(1)} %bitcast.7), channel_id=1, source_target_pairs={{0,1},{1,0},{2,3},{3,2},{4,5},{5,4},{6,7},{7,6},{8,9},{9,8},{10,11... | collective-permute-start | bytes 589832 | tf_op jit(solution)/shard_map/ppermute | solution.py:237
  54.7 54.9 %copy-start = (bf16[12,1408]{1,0:T(8,128)(2,1)S(1)}, bf16[12,1408]{1,0:T(8,128)(2,1)}, u32[]{:S(2)}) copy-start(bf16[12,1408]{1,0:T(8,128)(2,1)} %win_ref.1) | copy-start | bytes 101380
  83.1 0.7 collective-permute-start.2

commit v4 on v2

--- a/solution.py
+++ b/solution.py
@@ -54,7 +54,7 @@
     steps, few, core_ref, amp_hbm, win_hbm, coef_hbm, out_ref, amp_ref, win_ref, coef_ref, half_ref, sems
 ):
     total, pairs, _ = amp_hbm.shape
-    dests, padded, lanes = out_ref.shape
+    dests, packed, lanes = out_ref.shape
     blocks, _, mus = coef_ref.shape
     width = lanes - mus
     side = pairs // few
@@ -84,29 +84,30 @@
     win_copy.wait()
     win = repeated(win_ref[...], few, width)
     own = mod(row_ids(few), few) == mod(lane_ids(width), few)
-    out_ref[:, total:, :mus] = jnp.zeros((dests, padded - total, mus), BF16)
     for step in range(steps):
         copies[step].wait()
         if step + ahead < steps:
             copies[step + ahead].start()
         block = amp_ref[step * virt : (step + 1) * virt].reshape(rows, amp_ref.shape[2])
-        deep = 768
-        half = lax.dot_general(block[:, :deep], win[:, :deep], LANES, preferred_element_type=F32)
-        half += lax.dot_general(block[:, deep:], win[:, deep:], LANES, preferred_element_type=F32)
+        half = lax.dot_general(block, win, LANES, preferred_element_type=F32)
         half = half.astype(BF16).astype(F32).reshape(virt, side, few, width)
         for x in range(side):
             part = jnp.sum(jnp.where(own, half[:, x], 0.0), axis=1)
             half_ref[x, step * virt : (step + 1) * virt, :] = part
-        if step == 0:
-            for b in range(blocks):
-                coef_copies[b].wait()
-                for x in range(side):
-                    out_ref[b * side + x, :total, :mus] = coef_ref[b]
-    half_ref[:, total:, :] = jnp.zeros((side, padded - total, width), F32)
-    for x in range(side):
-        half = half_ref[x].astype(BF16)
-        for b in range(blocks):
-            out_ref[b * side + x, :, mus:] = half
+    cols = win_hbm.shape[0] * few
+    free = width - cols
+    for b in range(blocks):
+        coef_copies[b].wait()
+        coef = coef_ref[b].astype(F32)
+        for x in range(side):
+            half = half_ref[x]
+            rest = [coef[packed:, at : at + free] for at in range(0, mus, free)]
+            rest += [half[packed:, at : at + free] for at in range(0, cols, free)]
+            rest.append(jnp.zeros((packed - len(rest) * (total - packed), free), F32))
+            rest = jnp.concatenate(rest, axis=0)
+            half = jnp.concatenate([half[:packed, :cols], rest], axis=1)
+            out_ref[b * side + x, :, :mus] = coef[:packed].astype(BF16)
+            out_ref[b * side + x, :, mus:] = half.astype(BF16)
 
 
 def amp_of(nuw, few, half, coef):
@@ -121,21 +122,36 @@
     return lax.dot_general(pick, wide, LANES, preferred_element_type=F32)[:few].astype(BF16)
 
 
-def own_amp_kernel(nuw, in_ref, out_ref):
-    parts, padded, lanes = in_ref.shape
+def unpack_kernel(cols, last, in_ref, coef_ref, half_ref):
+    parts, packed, lanes = in_ref.shape
     mus = lanes // 2
-    coef = in_ref[:, :, :mus].reshape(parts * padded, mus)
-    half = in_ref[:, :, mus:].reshape(parts * padded, mus)
+    free = mus - cols
+    whole = in_ref[...].astype(F32)
+    rest = whole[:, :, mus + cols :]
+    none = jnp.zeros((parts, coef_ref.shape[1] - packed - last, mus), F32)
+    count = mus // free
+    coef = [rest[:, i * last : (i + 1) * last] for i in range(count)]
+    coef = jnp.concatenate([whole[:, :, :mus], jnp.concatenate(coef, axis=2), none], axis=1)
+    coef_ref[...] = coef.astype(BF16)
+    half = [rest[:, i * last : (i + 1) * last] for i in range(count, count + cols // free)]
+    half.append(jnp.zeros((parts, last, free), F32))
+    half = jnp.concatenate([whole[:, :, mus:], jnp.concatenate(half, axis=2), none], axis=1)
+    half_ref[...] = half.astype(BF16)
+
+
+def own_amp_kernel(nuw, half_ref, coef_ref, out_ref):
+    parts, padded, mus = coef_ref.shape
+    coef = coef_ref[...].reshape(parts * padded, mus)
+    half = half_ref[...].reshape(parts * padded, mus)
     out_ref[...] = amp_of(nuw, out_ref.shape[0], half, coef)
 
 
-def amp_kernel(nuw, core_ref, in_ref, coef_ref, own_ref, out_ref):
-    parts, padded, lanes = in_ref.shape
+def amp_kernel(nuw, core_ref, half_ref, coef_ref, own_ref, out_ref):
+    parts, padded, mus = coef_ref.shape
     dests, few, cols = out_ref.shape
-    mus = lanes // 2
     repeat = dests * cols // (2 * mus * nuw)
     blocks = dests // (2 * repeat)
-    half = in_ref[:, :, mus:].reshape(parts * padded, mus)
+    half = half_ref[...].reshape(parts * padded, mus)
     other_amp = amp_of(nuw, few, half, coef_ref[...].reshape(parts * padded, mus))
     for other, amp in enumerate([own_ref[...], other_amp]):
         for b in range(blocks):
@@ -145,23 +161,18 @@
 
 
 def terms_kernel(blk, mask_ref, core_ref, amp_ref, other_amp_ref, ints_ref, out_ref, all_ref):
-    step = pl.program_id(0)
     rows, cols = ints_ref.shape
     dests, few, _ = out_ref.shape
     half = amp_ref.shape[0]
     side = 4
-
-    @pl.when(step == 0)
-    def _():
-        at = pl.multiple_of(core_ref[0] * half, half)
-        all_ref[pl.ds(at, half), :] = amp_ref[...]
-        at = pl.multiple_of((core_ref[0] ^ 1) * half, half)
-        all_ref[pl.ds(at, half), :] = other_amp_ref[...]
-
+    at = pl.multiple_of(core_ref[0] * half, half)
+    all_ref[pl.ds(at, half), :] = amp_ref[...]
+    at = pl.multiple_of((core_ref[0] ^ 1) * half, half)
+    all_ref[pl.ds(at, half), :] = other_amp_ref[...]
     for col in range(cols // blk):
         total = None
         for row in range(rows // blk):
-            keep = mask_ref[row, step * (cols // blk) + col].astype(F32)
+            keep = mask_ref[row, col].astype(F32)
             term = keep * mm(
                 all_ref[:, row * blk : (row + 1) * blk],
                 ints_ref[row * blk : (row + 1) * blk, col * blk : (col + 1) * blk],
@@ -180,8 +191,9 @@
     out_ref[...] = total.astype(BF16)
 
 
-def forward_kernel(nuw, core_ref, in_ref, coef_ref, lad_ref, out_ref, order_ref):
-    dests, padded, lanes = out_ref.shape
+def forward_kernel(nuw, last, core_ref, coef_ref, other_coef_ref, lad_ref, out_ref, order_ref):
+    dests, packed, lanes = out_ref.shape
+    padded = coef_ref.shape[1]
     few, cols = lad_ref.shape
     mus = cols // nuw // 2
     part_cols = 384
@@ -198,16 +210,25 @@
         order_ref[part * run : (part + 1) * run, :] = some.astype(BF16)
     fwd = None
     for other in range(2):
-        coef = coef_ref[...] if other else in_ref[:, :, :mus]
+        coef = (other_coef_ref if other else coef_ref)[...]
         start = pl.multiple_of((core_ref[0] ^ other) * mus, mus)
         part = mm(coef.reshape(dests * padded, mus), order_ref[pl.ds(start, mus), :])
         fwd = part if fwd is None else fwd + part
-    out_ref[...] = fwd.astype(BF16).reshape(out_ref.shape)
+    fwd = fwd.reshape(dests, padded, lanes)
+    used = nuw * few
+    free = lanes - used
+    rest = [fwd[:, packed : packed + last, at : at + free] for at in range(0, used, free)]
+    rest.append(jnp.zeros((dests, packed - len(rest) * last, free), F32))
+    fwd = jnp.concatenate([fwd[:, :packed, :used], jnp.concatenate(rest, axis=1)], axis=2)
+    out_ref[...] = fwd.astype(BF16)
 
 
 def out_kernel(steps, few, fwd_ref, win_ref, out_hbm, out_ref, sems):
-    parts, _, lanes = fwd_ref.shape
+    parts, packed, lanes = fwd_ref.shape
     total, pairs, nv = out_ref.shape
+    last = total - packed
+    used = win_ref.shape[0] * few
+    free = lanes - used
     side = pairs // few
     virt = total // steps
     win = repeated(win_ref[...], few, lanes)
@@ -218,7 +239,9 @@
         for block in range(parts // side):
             part = fwd_ref[block * side + x].astype(F32)
             fwd = part if fwd is None else fwd + part
-        fwds.append(fwd)
+        rest = [fwd[i * last : (i + 1) * last, used:] for i in range(used // free)]
+        rest.append(jnp.zeros((last, free), F32))
+        fwds.append(jnp.concatenate([fwd, jnp.concatenate(rest, axis=1)], axis=0))
     copies = []
     for step in range(steps):
         cut = slice(step * virt, (step + 1) * virt)
@@ -262,7 +285,7 @@
     mus = nao * side // sp
     width = 128
     steps = 4
-    padded = -(-virt // 16) * 16
+    padded, packed = -(-virt // 16) * 16, virt // 8 * 8
     amp = jnp.transpose(amplitudes, (1, 0, 2))
     coef = jnp.transpose(virtual_coef, (1, 0))
     my_core = lax.axis_index("core").reshape(1)
@@ -274,26 +297,32 @@
         functools.partial(half_kernel, steps, few),
         in_specs=[smem, hbm, hbm, hbm],
         out_specs=vmem,
-        out_shape=jax.ShapeDtypeStruct((sp, padded, mus // 2 + width), BF16),
+        out_shape=jax.ShapeDtypeStruct((sp, packed, mus // 2 + width), BF16),
         scratch_shapes=[
             pltpu.VMEM((virt, pairs, nv), BF16),
             pltpu.VMEM((nuw, nv), BF16),
             pltpu.VMEM((nao // mus, virt, mus // 2), BF16),
-            pltpu.VMEM((side, padded, width), F32),
+            pltpu.VMEM((side, virt, width), F32),
             pltpu.SemaphoreType.DMA((steps + 1 + nao // mus,)),
         ],
         compiler_params=params(54),
         name="half",
     )(my_core, amp, window_coef, coef)
     chunk = exchange(sent, ("y", "z", "x"))
-    other_coef = swap(chunk[:, :, : mus // 2], "core")
+    own_coef, half = pl.pallas_call(
+        functools.partial(unpack_kernel, nuw * few, virt - packed),
+        out_shape=[jax.ShapeDtypeStruct((sp, padded, width), BF16)] * 2,
+        compiler_params=params(),
+        name="unpack",
+    )(chunk)
+    other_coef = swap(own_coef, "core")
     flat = sizes["x"] * sizes["zh"]
     own_amp = pl.pallas_call(
         functools.partial(own_amp_kernel, nuw),
         out_shape=jax.ShapeDtypeStruct((few, mus // 2 * nuw), BF16),
         compiler_params=params(),
         name="own_amp",
-    )(chunk)
+    )(half, own_coef)
     ao_amp = pl.pallas_call(
         functools.partial(amp_kernel, nuw),
         in_specs=[smem, vmem, vmem, vmem],
@@ -301,26 +330,17 @@
         out_shape=jax.ShapeDtypeStruct((flat, few, rows), BF16),
         compiler_params=params(),
         name="amp",
-    )(my_core, chunk, other_coef, own_amp)
+    )(my_core, half, other_coef, own_amp)
     amp_here = exchange(ao_amp, ("x", "zh")).reshape(flat * few, rows)
     amp_there = swap(amp_here, "core")
 
-    wide = cols // 4
-    whole = lambda array: pl.BlockSpec(array.shape, lambda i: (0, 0))
     terms = pl.pallas_call(
         functools.partial(terms_kernel, rows // block_mask.shape[0]),
-        grid=(cols // wide,),
-        in_specs=[
-            smem,
-            smem,
-            whole(amp_here),
-            whole(amp_there),
-            pl.BlockSpec((rows, wide), lambda i: (0, i)),
-        ],
-        out_specs=pl.BlockSpec((sp, few, wide), lambda i: (0, 0, i)),
+        in_specs=[smem, smem, vmem, vmem, vmem],
+        out_specs=vmem,
         out_shape=jax.ShapeDtypeStruct((sp, few, cols), BF16),
         scratch_shapes=[pltpu.VMEM((op * pairs, rows), BF16)],
-        compiler_params=params(24),
+        compiler_params=params(),
         name="terms",
     )(block_mask, my_core, amp_here, amp_there, integrals)
     pieces = exchange(terms, ("y", "z", "x"))
@@ -332,14 +352,14 @@
     )(pieces)
     owned = turn(ladder, sizes)
     fwd = pl.pallas_call(
-        functools.partial(forward_kernel, nuw),
+        functools.partial(forward_kernel, nuw, virt - packed),
         in_specs=[smem, vmem, vmem, vmem],
         out_specs=vmem,
-        out_shape=jax.ShapeDtypeStruct((sp, padded, width), BF16),
+        out_shape=jax.ShapeDtypeStruct((sp, packed, width), BF16),
         scratch_shapes=[pltpu.VMEM((mus, width), BF16)],
         compiler_params=params(),
         name="forward",
-    )(my_core, chunk, other_coef, owned)
+    )(my_core, own_coef, other_coef, owned)
     fwd = exchange(fwd, ("y", "z", "x"))
     out = pl.pallas_call(
         functools.partial(out_kernel, steps, few),

time: 112 us -> 110 us (0.982)
  blocking collectives: 94.9 us -> 93 us
    all_to_all x4, blocking collectives: 94.9 us -> 93 us  [exchange(): return lax.all_to_all(array, axes, split_axis=0, concat_axis=0, tiled=True)]
where the time goes in v4:
time: 110 us
  blocking collectives  93 us (85%)
  Pallas kernels  13.7 us (12%)
  waiting for transfers between devices  2.39 us (2%)
    all_to_all x4, blocking collectives, exchange(): return lax.all_to_all(array, axes, split_axis=0, concat_axis=0, tiled=True)  93 us
    pallas_call x1, Pallas kernels, local(): pl.pallas_call(functools.partial(half_kernel, steps, few), in_specs=[smem...  6.23 us
    pallas_call x1, Pallas kernels, local(): pl.pallas_call(functools.partial(out_kernel, steps, few), in_specs=[vmem,...  2.41 us
    ppermute x2, waiting for transfers between devices, swap(): return lax.ppermute(array, axis, [(0, 1), (1, 0)])  2.38 us
  transfers between devices with their start and end apart: 3, of which 2 were waited for; matrix products, arithmetic and copies ran while one was open for 0% of the time, Pallas kernels for 1%

profile of v4, /device:TPU:2, one launch (start us, length us, event | category | flops | bytes accessed | tf_op | source)
XLA Modules:
  0.0 109.9 jit_solution(1781342071920375089)
XLA Ops:
  0.0 0.0 slice-start
  0.0 0.0 slice-start.1
  0.0 0.0 copy-start.1
  0.0 6.2 %half.1 = bf16[32,40,256]{2,1,0:T(8,128)(2,1)} custom-call(s32[1]{0:T(128)} %bitcast.core_ref, bf16[44,32,1408]{2,1,0:T(8,128)(2,1)} %bitcast.9, bf16[12,1408]{1,0:T(8,128)(2,1)} %win_ref.1, bf16[44,2048]{1,0:T(8,128)(2,1)} %bitcast.10), custom_call_target="tpu_custom_call" | custom-call | tf_op jit(solution)/shard_map/half/pallas_call | solution.py:296
  6.3 21.1 %all_to_all.20.in_ref = bf16[32,40,256]{2,1,0:T(8,128)(2,1)S(1)} all-to-all(bf16[32,40,256]{2,1,0:T(8,128)(2,1)} %half.1), channel_id=1, replica_groups=mesh['y'=4,'z'=2,'x'=4,'zh'=4,'core'=2] {'y','z','x'}, dimensions={0} | all-to-all | bytes 1310720 | tf_op jit(solution)/shard_map/all_to_all | solution.py:273
  27.4 0.2 unpack.1
  27.6 0.1 collective-permute-start
  27.7 0.8 own_amp.1.own_ref
  28.5 0.9 collective-permute-done.coef_ref.other_coef_ref
  29.4 0.8 amp.1
  30.2 19.4 %all_to_all.21 = bf16[16,8,768]{2,1,0:T(8,128)(2,1)S(1)} all-to-all(bf16[16,8,768]{2,1,0:T(8,128)(2,1)S(1)} %amp.1), channel_id=1, replica_groups=mesh['y'=4,'z'=2,'x'=4,'zh'=4,'core'=2] {'x','zh'}, dimensions={0} | all-to-all | bytes 393216 | tf_op jit(solution)/shard_map/all_to_all | solution.py:273
  49.6 0.0 collective-permute-start.1
  49.6 1.4 %collective-permute-done.1.other_amp_ref = bf16[128,768]{1,0:T(8,128)(2,1)S(1)} collective-permute-done((bf16[128,768]{1,0:T(8,128)(2,1)S(1)}, bf16[128,768]{1,0:T(8,128)(2,1)S(1)}, u32[]{:S(2)}, u32[]{:S(2)}) %collective-permute-start.1) | collective-permute-done | bytes 196640 | tf_op jit(solution)/shard_map/ppermute | solution.py:263
  51.0 0.0 slice-done
  51.0 0.0 slice-done.1
  51.0 0.0 copy-done.1
  51.0 2.0 %terms.1 = bf16[32,8,3072]{2,1,0:T(8,128)(2,1)S(1)} custom-call(s32[3,12]{1,0:T(4,128)S(1)} %copy-done.1, s32[1]{0:T(128)} %bitcast.core_ref, bf16[128,768]{1,0:T(8,128)(2,1)S(1)} %bitcast.8, bf16[128,768]{1,0:T(8,128)(2,1)S(1)} %collective-permute-done.1.other_amp_ref, bf16[768,3072]{1,0:T(8,128)(2,1)S(1)} %bitcast.6), custom_call_target="tpu_custom_call" | custom-call | tf_op jit(solution)/shard_map/terms/pallas_call | solution.py:337
  53.0 0.0 copy-start
  53.0 28.2 %all_to_all.22.in_ref = bf16[32,8,3072]{2,1,0:T(8,128)(2,1)S(1)} all-to-all(bf16[32,8,3072]{2,1,0:T(8,128)(2,1)S(1)} %terms.1), channel_id=1, replica_groups=mesh['y'=4,'z'=2,'x'=4,'zh'=4,'core'=2] {'y','z','x'}, dimensions={0} | all-to-all | bytes 3145728 | tf_op jit(solution)/shard_map/all_to_all | solution.py:273
  81.2 0.2 sum_terms.1
  81.4 0.7 collective-permute-start.2
  82.1 0.0 collective-permute-done.2.lad_ref
  82.1 1.1 forward.1
  83.2 24.3 %all_to_all.23.fwd_ref = bf16[32,40,128]{2,1,0:T(8,128)(2,1)S(1)} all-to-all(bf16[32,40,128]{2,1,0:T(8,128)(2,1)S(1)} %forward.1), channel_id=1, replica_groups=mesh['y'=4,'z'=2,'x'=4,'zh'=4,'core'=2] {'y','z','x'}, dimensions={0} | all-to-all | bytes 655360 | tf_op jit(solution)/shard_map/all_to_all | solution.py:273
  107.5 0.0 copy-done
  107.5 2.4 %out.1 = bf16[44,32,1408]{2,1,0:T(8,128)(2,1)} custom-call(bf16[32,40,128]{2,1,0:T(8,128)(2,1)S(1)} %all_to_all.23.fwd_ref, bf16[12,1408]{1,0:T(8,128)(2,1)S(1)} %copy-done), custom_call_target="tpu_custom_call" | custom-call | tf_op jit(solution)/shard_map/out/pallas_call | solution.py:364
  (1 shorter events, 0.0 us)
Async XLA Ops:
  0.0 51.0 %slice-start = ((s8[4718592]{0:T(1024)(128)(4,1)}), s8[4194304]{0:T(1024)(128)(4,1)S(1)}, s32[]{:S(2)}) async-start(s8[4718592]{0:T(1024)(128)(4,1)} %bitcast.5), calls=%async_computation.4 | async-start | bytes 8388608
  0.0 51.0 %slice-start.1 = ((s8[4718592]{0:T(1024)(128)(4,1)}), s8[524288]{0:T(1024)(128)(4,1)S(1)}, s32[]{:S(2)}) async-start(s8[4718592]{0:T(1024)(128)(4,1)} %bitcast.5), calls=%async_computation.5 | async-start | bytes 1048576
  0.0 51.0 %copy-start.1 = (s32[3,12]{1,0:T(4,128)S(1)}, s32[3,12]{1,0:T(4,128)}, u32[]{:S(2)}) copy-start(s32[3,12]{1,0:T(4,128)} %mask_ref.1) | copy-start | bytes 436
  27.6 1.8 %collective-permute-start = (bf16[32,48,128]{2,1,0:T(8,128)(2,1)S(1)}, bf16[32,48,128]{2,1,0:T(8,128)(2,1)S(1)}, u32[]{:S(2)}, u32[]{:S(2)}) collective-permute-start(bf16[32,48,128]{2,1,0:T(8,128)(2,1)S(1)} %get-tuple-element.7.coef_ref), channel_id=1, source_target_pairs={{0,1},{1,0},{2,3},{3,2},{4,5},{5,4},{6,7},{7,6},{8,9},{9,8},{10,11... | collective-permute-start | bytes 1179656 | tf_op jit(solution)/shard_map/ppermute | solution.py:263
  49.6 1.4 %collective-permute-start.1 = (bf16[128,768]{1,0:T(8,128)(2,1)S(1)}, bf16[128,768]{1,0:T(8,128)(2,1)S(1)}, u32[]{:S(2)}, u32[]{:S(2)}) collective-permute-start(bf16[128,768]{1,0:T(8,128)(2,1)S(1)} %bitcast.7), channel_id=1, source_target_pairs={{0,1},{1,0},{2,3},{3,2},{4,5},{5,4},{6,7},{7,6},{8,9},{9,8},{10,11... | collective-permute-start | bytes 589832 | tf_op jit(solution)/shard_map/ppermute | solution.py:263
  53.0 54.5 %copy-start = (bf16[12,1408]{1,0:T(8,128)(2,1)S(1)}, bf16[12,1408]{1,0:T(8,128)(2,1)}, u32[]{:S(2)}) copy-start(bf16[12,1408]{1,0:T(8,128)(2,1)} %win_ref.1) | copy-start | bytes 101380
  81.4 0.7 collective-permute-start.2

commit v5 on v4

--- a/solution.py
+++ b/solution.py
@@ -51,13 +51,16 @@
 
 
 def half_kernel(
-    steps, few, core_ref, amp_hbm, win_hbm, coef_hbm, out_ref, amp_ref, win_ref, coef_ref, half_ref, sems
+    steps, few, core_ref, amp_hbm, win_hbm, coef_hbm, out_ref, amp_ref, win_ref, coef_ref, half_ref, rest_ref, sems
 ):
     total, pairs, _ = amp_hbm.shape
     dests, packed, lanes = out_ref.shape
     blocks, _, mus = coef_ref.shape
     width = lanes - mus
     side = pairs // few
+    last = total - packed
+    cols = win_hbm.shape[0] * few
+    free = width - cols
     virt = total // steps
     rows = virt * pairs
     ahead = 3
@@ -94,20 +97,27 @@
         for x in range(side):
             part = jnp.sum(jnp.where(own, half[:, x], 0.0), axis=1)
             half_ref[x, step * virt : (step + 1) * virt, :] = part
-    cols = win_hbm.shape[0] * few
-    free = width - cols
-    for b in range(blocks):
-        coef_copies[b].wait()
-        coef = coef_ref[b].astype(F32)
-        for x in range(side):
-            half = half_ref[x]
-            rest = [coef[packed:, at : at + free] for at in range(0, mus, free)]
-            rest += [half[packed:, at : at + free] for at in range(0, cols, free)]
-            rest.append(jnp.zeros((packed - len(rest) * (total - packed), free), F32))
-            rest = jnp.concatenate(rest, axis=0)
-            half = jnp.concatenate([half[:packed, :cols], rest], axis=1)
-            out_ref[b * side + x, :, :mus] = coef[:packed].astype(BF16)
-            out_ref[b * side + x, :, mus:] = half.astype(BF16)
+        if step == 0:
+            for b in range(blocks):
+                coef_copies[b].wait()
+                coef = coef_ref[b].astype(F32)
+                rest = [coef[packed:, at : at + free] for at in range(0, mus, free)]
+                rest = jnp.concatenate(rest, axis=0)
+                rest_ref[b] = jnp.concatenate([jnp.zeros((rest.shape[0], cols), F32), rest], axis=1)
+                for x in range(side):
+                    out_ref[b * side + x, :, :mus] = coef[:packed].astype(BF16)
+    halves = []
+    for x in range(side):
+        half = half_ref[x]
+        rest = [jnp.zeros((mus // free * last, free), F32)]
+        rest += [half[packed:, at : at + free] for at in range(0, cols, free)]
+        rest.append(jnp.zeros((packed - (mus + cols) // free * last, free), F32))
+        halves.append(jnp.concatenate([half[:packed, :cols], jnp.concatenate(rest, axis=0)], axis=1))
+    for x in range(side):
+        low = halves[x][mus // free * last :].astype(BF16)
+        for b in range(blocks):
+            high = (halves[x][: mus // free * last] + rest_ref[b]).astype(BF16)
+            out_ref[b * side + x, :, mus:] = jnp.concatenate([high, low], axis=0)
 
 
 def amp_of(nuw, few, half, coef):
@@ -303,6 +313,7 @@
             pltpu.VMEM((nuw, nv), BF16),
             pltpu.VMEM((nao // mus, virt, mus // 2), BF16),
             pltpu.VMEM((side, virt, width), F32),
+            pltpu.VMEM((nao // mus, 16, width), F32),
             pltpu.SemaphoreType.DMA((steps + 1 + nao // mus,)),
         ],
         compiler_params=params(54),

time: 110 us -> 110 us (level)
  no operation moved by 1% of the time
where the time goes in v5:
time: 110 us
  blocking collectives  93 us (85%)
  Pallas kernels  13.6 us (12%)
  waiting for transfers between devices  2.38 us (2%)
    all_to_all x4, blocking collectives, exchange(): return lax.all_to_all(array, axes, split_axis=0, concat_axis=0, tiled=True)  93 us
    pallas_call x1, Pallas kernels, local(): pl.pallas_call(functools.partial(half_kernel, steps, few), in_specs=[smem...  6.16 us
    pallas_call x1, Pallas kernels, local(): pl.pallas_call(functools.partial(out_kernel, steps, few), in_specs=[vmem,...  2.41 us
    ppermute x2, waiting for transfers between devices, swap(): return lax.ppermute(array, axis, [(0, 1), (1, 0)])  2.38 us
  transfers between devices with their start and end apart: 3, of which 2 were waited for; matrix products, arithmetic and copies ran while one was open for 0% of the time, Pallas kernels for 1%

profile of v5, /device:TPU:2, one launch (start us, length us, event | category | flops | bytes accessed | tf_op | source)
XLA Modules:
  0.0 109.8 jit_solution(10553648012582422548)
XLA Ops:
  0.0 0.0 slice-start
  0.0 0.0 slice-start.1
  0.0 0.0 copy-start.1
  0.0 6.2 %half.1 = bf16[32,40,256]{2,1,0:T(8,128)(2,1)} custom-call(s32[1]{0:T(128)} %bitcast.core_ref, bf16[44,32,1408]{2,1,0:T(8,128)(2,1)} %bitcast.9, bf16[12,1408]{1,0:T(8,128)(2,1)} %win_ref.1, bf16[44,2048]{1,0:T(8,128)(2,1)} %bitcast.10), custom_call_target="tpu_custom_call" | custom-call | tf_op jit(solution)/shard_map/half/pallas_call | solution.py:306
  6.2 21.1 %all_to_all.20.in_ref = bf16[32,40,256]{2,1,0:T(8,128)(2,1)S(1)} all-to-all(bf16[32,40,256]{2,1,0:T(8,128)(2,1)} %half.1), channel_id=1, replica_groups=mesh['y'=4,'z'=2,'x'=4,'zh'=4,'core'=2] {'y','z','x'}, dimensions={0} | all-to-all | bytes 1310720 | tf_op jit(solution)/shard_map/all_to_all | solution.py:283
  27.3 0.2 unpack.1
  27.5 0.1 collective-permute-start
  27.6 0.8 own_amp.1.own_ref
  28.4 0.9 collective-permute-done.coef_ref.other_coef_ref
  29.3 0.8 amp.1
  30.1 19.4 %all_to_all.21 = bf16[16,8,768]{2,1,0:T(8,128)(2,1)S(1)} all-to-all(bf16[16,8,768]{2,1,0:T(8,128)(2,1)S(1)} %amp.1), channel_id=1, replica_groups=mesh['y'=4,'z'=2,'x'=4,'zh'=4,'core'=2] {'x','zh'}, dimensions={0} | all-to-all | bytes 393216 | tf_op jit(solution)/shard_map/all_to_all | solution.py:283
  49.5 0.0 collective-permute-start.1
  49.5 1.4 %collective-permute-done.1.other_amp_ref = bf16[128,768]{1,0:T(8,128)(2,1)S(1)} collective-permute-done((bf16[128,768]{1,0:T(8,128)(2,1)S(1)}, bf16[128,768]{1,0:T(8,128)(2,1)S(1)}, u32[]{:S(2)}, u32[]{:S(2)}) %collective-permute-start.1) | collective-permute-done | bytes 196640 | tf_op jit(solution)/shard_map/ppermute | solution.py:273
  50.9 0.0 slice-done
  50.9 0.0 slice-done.1
  50.9 0.0 copy-done.1
  50.9 2.0 %terms.1 = bf16[32,8,3072]{2,1,0:T(8,128)(2,1)S(1)} custom-call(s32[3,12]{1,0:T(4,128)S(1)} %copy-done.1, s32[1]{0:T(128)} %bitcast.core_ref, bf16[128,768]{1,0:T(8,128)(2,1)S(1)} %bitcast.8, bf16[128,768]{1,0:T(8,128)(2,1)S(1)} %collective-permute-done.1.other_amp_ref, bf16[768,3072]{1,0:T(8,128)(2,1)S(1)} %bitcast.6), custom_call_target="tpu_custom_call" | custom-call | tf_op jit(solution)/shard_map/terms/pallas_call | solution.py:348
  52.9 0.0 copy-start
  53.0 28.1 %all_to_all.22.in_ref = bf16[32,8,3072]{2,1,0:T(8,128)(2,1)S(1)} all-to-all(bf16[32,8,3072]{2,1,0:T(8,128)(2,1)S(1)} %terms.1), channel_id=1, replica_groups=mesh['y'=4,'z'=2,'x'=4,'zh'=4,'core'=2] {'y','z','x'}, dimensions={0} | all-to-all | bytes 3145728 | tf_op jit(solution)/shard_map/all_to_all | solution.py:283
  81.1 0.2 sum_terms.1
  81.3 0.7 collective-permute-start.2
  82.0 0.0 collective-permute-done.2.lad_ref
  82.0 1.1 forward.1
  83.1 24.3 %all_to_all.23.fwd_ref = bf16[32,40,128]{2,1,0:T(8,128)(2,1)S(1)} all-to-all(bf16[32,40,128]{2,1,0:T(8,128)(2,1)S(1)} %forward.1), channel_id=1, replica_groups=mesh['y'=4,'z'=2,'x'=4,'zh'=4,'core'=2] {'y','z','x'}, dimensions={0} | all-to-all | bytes 655360 | tf_op jit(solution)/shard_map/all_to_all | solution.py:283
  107.4 0.0 copy-done
  107.4 2.4 %out.1 = bf16[44,32,1408]{2,1,0:T(8,128)(2,1)} custom-call(bf16[32,40,128]{2,1,0:T(8,128)(2,1)S(1)} %all_to_all.23.fwd_ref, bf16[12,1408]{1,0:T(8,128)(2,1)S(1)} %copy-done), custom_call_target="tpu_custom_call" | custom-call | tf_op jit(solution)/shard_map/out/pallas_call | solution.py:375
  (1 shorter events, 0.0 us)
Async XLA Ops:
  0.0 50.9 %slice-start = ((s8[4718592]{0:T(1024)(128)(4,1)}), s8[4194304]{0:T(1024)(128)(4,1)S(1)}, s32[]{:S(2)}) async-start(s8[4718592]{0:T(1024)(128)(4,1)} %bitcast.5), calls=%async_computation.4 | async-start | bytes 8388608
  0.0 50.9 %slice-start.1 = ((s8[4718592]{0:T(1024)(128)(4,1)}), s8[524288]{0:T(1024)(128)(4,1)S(1)}, s32[]{:S(2)}) async-start(s8[4718592]{0:T(1024)(128)(4,1)} %bitcast.5), calls=%async_computation.5 | async-start | bytes 1048576
  0.0 50.9 %copy-start.1 = (s32[3,12]{1,0:T(4,128)S(1)}, s32[3,12]{1,0:T(4,128)}, u32[]{:S(2)}) copy-start(s32[3,12]{1,0:T(4,128)} %mask_ref.1) | copy-start | bytes 436
  27.5 1.8 %collective-permute-start = (bf16[32,48,128]{2,1,0:T(8,128)(2,1)S(1)}, bf16[32,48,128]{2,1,0:T(8,128)(2,1)S(1)}, u32[]{:S(2)}, u32[]{:S(2)}) collective-permute-start(bf16[32,48,128]{2,1,0:T(8,128)(2,1)S(1)} %get-tuple-element.7.coef_ref), channel_id=1, source_target_pairs={{0,1},{1,0},{2,3},{3,2},{4,5},{5,4},{6,7},{7,6},{8,9},{9,8},{10,11... | collective-permute-start | bytes 1179656 | tf_op jit(solution)/shard_map/ppermute | solution.py:273
  49.5 1.4 %collective-permute-start.1 = (bf16[128,768]{1,0:T(8,128)(2,1)S(1)}, bf16[128,768]{1,0:T(8,128)(2,1)S(1)}, u32[]{:S(2)}, u32[]{:S(2)}) collective-permute-start(bf16[128,768]{1,0:T(8,128)(2,1)S(1)} %bitcast.7), channel_id=1, source_target_pairs={{0,1},{1,0},{2,3},{3,2},{4,5},{5,4},{6,7},{7,6},{8,9},{9,8},{10,11... | collective-permute-start | bytes 589832 | tf_op jit(solution)/shard_map/ppermute | solution.py:273
  52.9 54.5 %copy-start = (bf16[12,1408]{1,0:T(8,128)(2,1)S(1)}, bf16[12,1408]{1,0:T(8,128)(2,1)}, u32[]{:S(2)}) copy-start(bf16[12,1408]{1,0:T(8,128)(2,1)} %win_ref.1) | copy-start | bytes 101380
  81.3 0.7 collective-permute-start.2

commit v6 on v5

--- a/solution.py
+++ b/solution.py
@@ -54,9 +54,9 @@
     steps, few, core_ref, amp_hbm, win_hbm, coef_hbm, out_ref, amp_ref, win_ref, coef_ref, half_ref, rest_ref, sems
 ):
     total, pairs, _ = amp_hbm.shape
-    dests, packed, lanes = out_ref.shape
+    dests, both, width = out_ref.shape
     blocks, _, mus = coef_ref.shape
-    width = lanes - mus
+    packed = both // 2
     side = pairs // few
     last = total - packed
     cols = win_hbm.shape[0] * few
@@ -103,9 +103,9 @@
                 coef = coef_ref[b].astype(F32)
                 rest = [coef[packed:, at : at + free] for at in range(0, mus, free)]
                 rest = jnp.concatenate(rest, axis=0)
-                rest_ref[b] = jnp.concatenate([jnp.zeros((rest.shape[0], cols), F32), rest], axis=1)
-                for x in range(side):
-                    out_ref[b * side + x, :, :mus] = coef[:packed].astype(BF16)
+                rest = jnp.concatenate([jnp.zeros((rest.shape[0], cols), F32), rest], axis=1)
+                rest_ref[b, :packed] = coef[:packed]
+                rest_ref[b, packed:] = rest
     halves = []
     for x in range(side):
         half = half_ref[x]
@@ -113,11 +113,12 @@
         rest += [half[packed:, at : at + free] for at in range(0, cols, free)]
         rest.append(jnp.zeros((packed - (mus + cols) // free * last, free), F32))
         halves.append(jnp.concatenate([half[:packed, :cols], jnp.concatenate(rest, axis=0)], axis=1))
-    for x in range(side):
-        low = halves[x][mus // free * last :].astype(BF16)
-        for b in range(blocks):
-            high = (halves[x][: mus // free * last] + rest_ref[b]).astype(BF16)
-            out_ref[b * side + x, :, mus:] = jnp.concatenate([high, low], axis=0)
+    high = mus // free * last
+    for b in range(blocks):
+        coef = rest_ref[b]
+        for x in range(side):
+            piece = [coef[:packed], coef[packed:] + halves[x][:high], halves[x][high:]]
+            out_ref[b * side + x] = jnp.concatenate(piece, axis=0).astype(BF16)
 
 
 def amp_of(nuw, few, half, coef):
@@ -133,19 +134,19 @@
 
 
 def unpack_kernel(cols, last, in_ref, coef_ref, half_ref):
-    parts, packed, lanes = in_ref.shape
-    mus = lanes // 2
+    parts, both, mus = in_ref.shape
+    packed = both // 2
     free = mus - cols
     whole = in_ref[...].astype(F32)
-    rest = whole[:, :, mus + cols :]
+    rest = whole[:, packed:, cols:]
     none = jnp.zeros((parts, coef_ref.shape[1] - packed - last, mus), F32)
     count = mus // free
     coef = [rest[:, i * last : (i + 1) * last] for i in range(count)]
-    coef = jnp.concatenate([whole[:, :, :mus], jnp.concatenate(coef, axis=2), none], axis=1)
+    coef = jnp.concatenate([whole[:, :packed], jnp.concatenate(coef, axis=2), none], axis=1)
     coef_ref[...] = coef.astype(BF16)
     half = [rest[:, i * last : (i + 1) * last] for i in range(count, count + cols // free)]
     half.append(jnp.zeros((parts, last, free), F32))
-    half = jnp.concatenate([whole[:, :, mus:], jnp.concatenate(half, axis=2), none], axis=1)
+    half = jnp.concatenate([whole[:, packed:], jnp.concatenate(half, axis=2), none], axis=1)
     half_ref[...] = half.astype(BF16)
 
 
@@ -307,13 +308,13 @@
         functools.partial(half_kernel, steps, few),
         in_specs=[smem, hbm, hbm, hbm],
         out_specs=vmem,
-        out_shape=jax.ShapeDtypeStruct((sp, packed, mus // 2 + width), BF16),
+        out_shape=jax.ShapeDtypeStruct((sp, 2 * packed, width), BF16),
         scratch_shapes=[
             pltpu.VMEM((virt, pairs, nv), BF16),
             pltpu.VMEM((nuw, nv), BF16),
             pltpu.VMEM((nao // mus, virt, mus // 2), BF16),
             pltpu.VMEM((side, virt, width), F32),
-            pltpu.VMEM((nao // mus, 16, width), F32),
+            pltpu.VMEM((nao // mus, packed + 16, width), F32),
             pltpu.SemaphoreType.DMA((steps + 1 + nao // mus,)),
         ],
         compiler_params=params(54),

time: 110 us -> 110 us (level)
  no operation moved by 1% of the time
where the time goes in v6:
time: 110 us
  blocking collectives  93 us (85%)
  Pallas kernels  13.6 us (12%)
  waiting for transfers between devices  2.38 us (2%)
    all_to_all x4, blocking collectives, exchange(): return lax.all_to_all(array, axes, split_axis=0, concat_axis=0, tiled=True)  93 us
    pallas_call x1, Pallas kernels, local(): pl.pallas_call(functools.partial(half_kernel, steps, few), in_specs=[smem...  6.13 us
    pallas_call x1, Pallas kernels, local(): pl.pallas_call(functools.partial(out_kernel, steps, few), in_specs=[vmem,...  2.41 us
    ppermute x2, waiting for transfers between devices, swap(): return lax.ppermute(array, axis, [(0, 1), (1, 0)])  2.38 us
  transfers between devices with their start and end apart: 3, of which 2 were waited for; matrix products, arithmetic and copies ran while one was open for 0% of the time, Pallas kernels for 1%

profile of v6, /device:TPU:2, one launch (start us, length us, event | category | flops | bytes accessed | tf_op | source)
XLA Modules:
  0.0 109.8 jit_solution(511445352277914202)
XLA Ops:
  0.0 0.0 slice-start
  0.0 0.0 slice-start.1
  0.0 0.0 copy-start.1
  0.0 6.1 %half.1 = bf16[32,80,128]{2,1,0:T(8,128)(2,1)} custom-call(s32[1]{0:T(128)} %bitcast.core_ref, bf16[44,32,1408]{2,1,0:T(8,128)(2,1)} %bitcast.9, bf16[12,1408]{1,0:T(8,128)(2,1)} %win_ref.1, bf16[44,2048]{1,0:T(8,128)(2,1)} %bitcast.10), custom_call_target="tpu_custom_call" | custom-call | tf_op jit(solution)/shard_map/half/pallas_call | solution.py:307
  6.1 21.1 %all_to_all.20.in_ref = bf16[32,80,128]{2,1,0:T(8,128)(2,1)S(1)} all-to-all(bf16[32,80,128]{2,1,0:T(8,128)(2,1)} %half.1), channel_id=1, replica_groups=mesh['y'=4,'z'=2,'x'=4,'zh'=4,'core'=2] {'y','z','x'}, dimensions={0} | all-to-all | bytes 1310720 | tf_op jit(solution)/shard_map/all_to_all | solution.py:284
  27.3 0.2 unpack.1
  27.5 0.1 collective-permute-start
  27.6 0.8 own_amp.1.own_ref
  28.4 0.9 collective-permute-done.coef_ref.other_coef_ref
  29.3 0.8 amp.1
  30.1 19.4 %all_to_all.21 = bf16[16,8,768]{2,1,0:T(8,128)(2,1)S(1)} all-to-all(bf16[16,8,768]{2,1,0:T(8,128)(2,1)S(1)} %amp.1), channel_id=1, replica_groups=mesh['y'=4,'z'=2,'x'=4,'zh'=4,'core'=2] {'x','zh'}, dimensions={0} | all-to-all | bytes 393216 | tf_op jit(solution)/shard_map/all_to_all | solution.py:284
  49.5 0.0 collective-permute-start.1
  49.5 1.4 %collective-permute-done.1.other_amp_ref = bf16[128,768]{1,0:T(8,128)(2,1)S(1)} collective-permute-done((bf16[128,768]{1,0:T(8,128)(2,1)S(1)}, bf16[128,768]{1,0:T(8,128)(2,1)S(1)}, u32[]{:S(2)}, u32[]{:S(2)}) %collective-permute-start.1) | collective-permute-done | bytes 196640 | tf_op jit(solution)/shard_map/ppermute | solution.py:274
  50.9 0.0 slice-done
  50.9 0.0 slice-done.1
  50.9 0.0 copy-done.1
  50.9 2.0 %terms.1 = bf16[32,8,3072]{2,1,0:T(8,128)(2,1)S(1)} custom-call(s32[3,12]{1,0:T(4,128)S(1)} %copy-done.1, s32[1]{0:T(128)} %bitcast.core_ref, bf16[128,768]{1,0:T(8,128)(2,1)S(1)} %bitcast.8, bf16[128,768]{1,0:T(8,128)(2,1)S(1)} %collective-permute-done.1.other_amp_ref, bf16[768,3072]{1,0:T(8,128)(2,1)S(1)} %bitcast.6), custom_call_target="tpu_custom_call" | custom-call | tf_op jit(solution)/shard_map/terms/pallas_call | solution.py:349
  52.9 0.0 copy-start
  52.9 28.1 %all_to_all.22.in_ref = bf16[32,8,3072]{2,1,0:T(8,128)(2,1)S(1)} all-to-all(bf16[32,8,3072]{2,1,0:T(8,128)(2,1)S(1)} %terms.1), channel_id=1, replica_groups=mesh['y'=4,'z'=2,'x'=4,'zh'=4,'core'=2] {'y','z','x'}, dimensions={0} | all-to-all | bytes 3145728 | tf_op jit(solution)/shard_map/all_to_all | solution.py:284
  81.1 0.2 sum_terms.1
  81.3 0.7 collective-permute-start.2
  82.0 0.0 collective-permute-done.2.lad_ref
  82.0 1.1 forward.1
  83.1 24.3 %all_to_all.23.fwd_ref = bf16[32,40,128]{2,1,0:T(8,128)(2,1)S(1)} all-to-all(bf16[32,40,128]{2,1,0:T(8,128)(2,1)S(1)} %forward.1), channel_id=1, replica_groups=mesh['y'=4,'z'=2,'x'=4,'zh'=4,'core'=2] {'y','z','x'}, dimensions={0} | all-to-all | bytes 655360 | tf_op jit(solution)/shard_map/all_to_all | solution.py:284
  107.4 0.0 copy-done
  107.4 2.4 %out.1 = bf16[44,32,1408]{2,1,0:T(8,128)(2,1)} custom-call(bf16[32,40,128]{2,1,0:T(8,128)(2,1)S(1)} %all_to_all.23.fwd_ref, bf16[12,1408]{1,0:T(8,128)(2,1)S(1)} %copy-done), custom_call_target="tpu_custom_call" | custom-call | tf_op jit(solution)/shard_map/out/pallas_call | solution.py:376
  (1 shorter events, 0.0 us)
Async XLA Ops:
  0.0 50.9 %slice-start = ((s8[4718592]{0:T(1024)(128)(4,1)}), s8[4194304]{0:T(1024)(128)(4,1)S(1)}, s32[]{:S(2)}) async-start(s8[4718592]{0:T(1024)(128)(4,1)} %bitcast.5), calls=%async_computation.4 | async-start | bytes 8388608
  0.0 50.9 %slice-start.1 = ((s8[4718592]{0:T(1024)(128)(4,1)}), s8[524288]{0:T(1024)(128)(4,1)S(1)}, s32[]{:S(2)}) async-start(s8[4718592]{0:T(1024)(128)(4,1)} %bitcast.5), calls=%async_computation.5 | async-start | bytes 1048576
  0.0 50.9 %copy-start.1 = (s32[3,12]{1,0:T(4,128)S(1)}, s32[3,12]{1,0:T(4,128)}, u32[]{:S(2)}) copy-start(s32[3,12]{1,0:T(4,128)} %mask_ref.1) | copy-start | bytes 436
  27.5 1.8 %collective-permute-start = (bf16[32,48,128]{2,1,0:T(8,128)(2,1)S(1)}, bf16[32,48,128]{2,1,0:T(8,128)(2,1)S(1)}, u32[]{:S(2)}, u32[]{:S(2)}) collective-permute-start(bf16[32,48,128]{2,1,0:T(8,128)(2,1)S(1)} %get-tuple-element.7.coef_ref), channel_id=1, source_target_pairs={{0,1},{1,0},{2,3},{3,2},{4,5},{5,4},{6,7},{7,6},{8,9},{9,8},{10,11... | collective-permute-start | bytes 1179656 | tf_op jit(solution)/shard_map/ppermute | solution.py:274
  49.5 1.4 %collective-permute-start.1 = (bf16[128,768]{1,0:T(8,128)(2,1)S(1)}, bf16[128,768]{1,0:T(8,128)(2,1)S(1)}, u32[]{:S(2)}, u32[]{:S(2)}) collective-permute-start(bf16[128,768]{1,0:T(8,128)(2,1)S(1)} %bitcast.7), channel_id=1, source_target_pairs={{0,1},{1,0},{2,3},{3,2},{4,5},{5,4},{6,7},{7,6},{8,9},{9,8},{10,11... | collective-permute-start | bytes 589832 | tf_op jit(solution)/shard_map/ppermute | solution.py:274
  52.9 54.5 %copy-start = (bf16[12,1408]{1,0:T(8,128)(2,1)S(1)}, bf16[12,1408]{1,0:T(8,128)(2,1)}, u32[]{:S(2)}) copy-start(bf16[12,1408]{1,0:T(8,128)(2,1)} %win_ref.1) | copy-start | bytes 101380
  81.3 0.7 collective-permute-start.2

commit v7 on v6

--- a/solution.py
+++ b/solution.py
@@ -79,11 +79,22 @@
         coef_copies.append(
             pltpu.make_async_copy(coef_hbm.at[:, pl.ds(start, mus)], coef_ref.at[b], sems.at[steps + 1 + b])
         )
+    for copy in coef_copies:
+        copy.start()
     win_copy.start()
     for copy in copies[:ahead]:
         copy.start()
-    for copy in coef_copies:
-        copy.start()
+    high = mus // free * last
+    whole = packed // 16 * 16
+    for b in range(blocks):
+        coef_copies[b].wait()
+        coef = coef_ref[b].astype(F32)
+        rest = [coef[packed:, at : at + free] for at in range(0, mus, free)]
+        rest = jnp.concatenate(rest, axis=0)
+        rest = jnp.concatenate([jnp.zeros((high, cols), F32), rest], axis=1)
+        rest_ref[b] = jnp.concatenate([coef[whole:packed], rest], axis=0)
+        for x in range(side):
+            out_ref[b * side + x, :whole] = coef[:whole].astype(BF16)
     win_copy.wait()
     win = repeated(win_ref[...], few, width)
     own = mod(row_ids(few), few) == mod(lane_ids(width), few)
@@ -97,15 +108,6 @@
         for x in range(side):
             part = jnp.sum(jnp.where(own, half[:, x], 0.0), axis=1)
             half_ref[x, step * virt : (step + 1) * virt, :] = part
-        if step == 0:
-            for b in range(blocks):
-                coef_copies[b].wait()
-                coef = coef_ref[b].astype(F32)
-                rest = [coef[packed:, at : at + free] for at in range(0, mus, free)]
-                rest = jnp.concatenate(rest, axis=0)
-                rest = jnp.concatenate([jnp.zeros((rest.shape[0], cols), F32), rest], axis=1)
-                rest_ref[b, :packed] = coef[:packed]
-                rest_ref[b, packed:] = rest
     halves = []
     for x in range(side):
         half = half_ref[x]
@@ -113,12 +115,16 @@
         rest += [half[packed:, at : at + free] for at in range(0, cols, free)]
         rest.append(jnp.zeros((packed - (mus + cols) // free * last, free), F32))
         halves.append(jnp.concatenate([half[:packed, :cols], jnp.concatenate(rest, axis=0)], axis=1))
-    high = mus // free * last
-    for b in range(blocks):
-        coef = rest_ref[b]
-        for x in range(side):
-            piece = [coef[:packed], coef[packed:] + halves[x][:high], halves[x][high:]]
-            out_ref[b * side + x] = jnp.concatenate(piece, axis=0).astype(BF16)
+    left = packed - whole
+    middle = high + left
+    for x in range(side):
+        low = halves[x][middle:].astype(BF16)
+        for b in range(blocks):
+            rest = rest_ref[b]
+            piece = [rest[:left], rest[left:] + halves[x][:high], halves[x][high:middle]]
+            piece = jnp.concatenate(piece, axis=0).astype(BF16)
+            out_ref[b * side + x, whole : packed + middle] = piece
+            out_ref[b * side + x, packed + middle :] = low
 
 
 def amp_of(nuw, few, half, coef):
@@ -314,7 +320,7 @@
             pltpu.VMEM((nuw, nv), BF16),
             pltpu.VMEM((nao // mus, virt, mus // 2), BF16),
             pltpu.VMEM((side, virt, width), F32),
-            pltpu.VMEM((nao // mus, packed + 16, width), F32),
+            pltpu.VMEM((nao // mus, packed % 16 + 16, width), F32),
             pltpu.SemaphoreType.DMA((steps + 1 + nao // mus,)),
         ],
         compiler_params=params(54),

time: 110 us -> 110 us (level)
  no operation moved by 1% of the time
where the time goes in v7:
time: 110 us; the launch traced here: 109 us
  blocking collectives  93 us (85%)
  Pallas kernels  13.1 us (12%)
  waiting for transfers between devices  2.38 us (2%)
    all_to_all x4, blocking collectives, exchange(): return lax.all_to_all(array, axes, split_axis=0, concat_axis=0, tiled=True)  93 us
    pallas_call x1, Pallas kernels, local(): pl.pallas_call(functools.partial(half_kernel, steps, few), in_specs=[smem...  5.66 us
    pallas_call x1, Pallas kernels, local(): pl.pallas_call(functools.partial(out_kernel, steps, few), in_specs=[vmem,...  2.41 us
    ppermute x2, waiting for transfers between devices, swap(): return lax.ppermute(array, axis, [(0, 1), (1, 0)])  2.38 us
  transfers between devices with their start and end apart: 3, of which 2 were waited for; matrix products, arithmetic and copies ran while one was open for 0% of the time, Pallas kernels for 1%

profile of v7, /device:TPU:2, one launch (start us, length us, event | category | flops | bytes accessed | tf_op | source)
XLA Modules:
  0.0 109.4 jit_solution(11674197137125337265)
XLA Ops:
  0.0 0.0 slice-start
  0.0 0.0 slice-start.1
  0.0 0.0 copy-start.1
  0.0 5.7 %half.1 = bf16[32,80,128]{2,1,0:T(8,128)(2,1)} custom-call(s32[1]{0:T(128)} %bitcast.core_ref, bf16[44,32,1408]{2,1,0:T(8,128)(2,1)} %bitcast.9, bf16[12,1408]{1,0:T(8,128)(2,1)} %win_ref.1, bf16[44,2048]{1,0:T(8,128)(2,1)} %bitcast.10), custom_call_target="tpu_custom_call" | custom-call | tf_op jit(solution)/shard_map/half/pallas_call | solution.py:313
  5.7 21.1 %all_to_all.20.in_ref = bf16[32,80,128]{2,1,0:T(8,128)(2,1)S(1)} all-to-all(bf16[32,80,128]{2,1,0:T(8,128)(2,1)} %half.1), channel_id=1, replica_groups=mesh['y'=4,'z'=2,'x'=4,'zh'=4,'core'=2] {'y','z','x'}, dimensions={0} | all-to-all | bytes 1310720 | tf_op jit(solution)/shard_map/all_to_all | solution.py:290
  26.8 0.2 unpack.1
  27.0 0.1 collective-permute-start
  27.1 0.8 own_amp.1.own_ref
  27.9 0.9 collective-permute-done.coef_ref.other_coef_ref
  28.8 0.8 amp.1
  29.6 19.4 %all_to_all.21 = bf16[16,8,768]{2,1,0:T(8,128)(2,1)S(1)} all-to-all(bf16[16,8,768]{2,1,0:T(8,128)(2,1)S(1)} %amp.1), channel_id=1, replica_groups=mesh['y'=4,'z'=2,'x'=4,'zh'=4,'core'=2] {'x','zh'}, dimensions={0} | all-to-all | bytes 393216 | tf_op jit(solution)/shard_map/all_to_all | solution.py:290
  49.0 0.0 collective-permute-start.1
  49.0 1.4 %collective-permute-done.1.other_amp_ref = bf16[128,768]{1,0:T(8,128)(2,1)S(1)} collective-permute-done((bf16[128,768]{1,0:T(8,128)(2,1)S(1)}, bf16[128,768]{1,0:T(8,128)(2,1)S(1)}, u32[]{:S(2)}, u32[]{:S(2)}) %collective-permute-start.1) | collective-permute-done | bytes 196640 | tf_op jit(solution)/shard_map/ppermute | solution.py:280
  50.4 0.0 slice-done
  50.4 0.0 slice-done.1
  50.4 0.0 copy-done.1
  50.5 2.0 %terms.1 = bf16[32,8,3072]{2,1,0:T(8,128)(2,1)S(1)} custom-call(s32[3,12]{1,0:T(4,128)S(1)} %copy-done.1, s32[1]{0:T(128)} %bitcast.core_ref, bf16[128,768]{1,0:T(8,128)(2,1)S(1)} %bitcast.8, bf16[128,768]{1,0:T(8,128)(2,1)S(1)} %collective-permute-done.1.other_amp_ref, bf16[768,3072]{1,0:T(8,128)(2,1)S(1)} %bitcast.6), custom_call_target="tpu_custom_call" | custom-call | tf_op jit(solution)/shard_map/terms/pallas_call | solution.py:355
  52.5 0.0 copy-start
  52.5 28.2 %all_to_all.22.in_ref = bf16[32,8,3072]{2,1,0:T(8,128)(2,1)S(1)} all-to-all(bf16[32,8,3072]{2,1,0:T(8,128)(2,1)S(1)} %terms.1), channel_id=1, replica_groups=mesh['y'=4,'z'=2,'x'=4,'zh'=4,'core'=2] {'y','z','x'}, dimensions={0} | all-to-all | bytes 3145728 | tf_op jit(solution)/shard_map/all_to_all | solution.py:290
  80.6 0.2 sum_terms.1
  80.8 0.7 collective-permute-start.2
  81.5 0.0 collective-permute-done.2.lad_ref
  81.5 1.1 forward.1
  82.6 24.3 %all_to_all.23.fwd_ref = bf16[32,40,128]{2,1,0:T(8,128)(2,1)S(1)} all-to-all(bf16[32,40,128]{2,1,0:T(8,128)(2,1)S(1)} %forward.1), channel_id=1, replica_groups=mesh['y'=4,'z'=2,'x'=4,'zh'=4,'core'=2] {'y','z','x'}, dimensions={0} | all-to-all | bytes 655360 | tf_op jit(solution)/shard_map/all_to_all | solution.py:290
  106.9 0.0 copy-done
  106.9 2.4 %out.1 = bf16[44,32,1408]{2,1,0:T(8,128)(2,1)} custom-call(bf16[32,40,128]{2,1,0:T(8,128)(2,1)S(1)} %all_to_all.23.fwd_ref, bf16[12,1408]{1,0:T(8,128)(2,1)S(1)} %copy-done), custom_call_target="tpu_custom_call" | custom-call | tf_op jit(solution)/shard_map/out/pallas_call | solution.py:382
  (1 shorter events, 0.0 us)
Async XLA Ops:
  0.0 50.4 %slice-start = ((s8[4718592]{0:T(1024)(128)(4,1)}), s8[4194304]{0:T(1024)(128)(4,1)S(1)}, s32[]{:S(2)}) async-start(s8[4718592]{0:T(1024)(128)(4,1)} %bitcast.5), calls=%async_computation.4 | async-start | bytes 8388608
  0.0 50.4 %slice-start.1 = ((s8[4718592]{0:T(1024)(128)(4,1)}), s8[524288]{0:T(1024)(128)(4,1)S(1)}, s32[]{:S(2)}) async-start(s8[4718592]{0:T(1024)(128)(4,1)} %bitcast.5), calls=%async_computation.5 | async-start | bytes 1048576
  0.0 50.4 %copy-start.1 = (s32[3,12]{1,0:T(4,128)S(1)}, s32[3,12]{1,0:T(4,128)}, u32[]{:S(2)}) copy-start(s32[3,12]{1,0:T(4,128)} %mask_ref.1) | copy-start | bytes 436
  27.0 1.8 %collective-permute-start = (bf16[32,48,128]{2,1,0:T(8,128)(2,1)S(1)}, bf16[32,48,128]{2,1,0:T(8,128)(2,1)S(1)}, u32[]{:S(2)}, u32[]{:S(2)}) collective-permute-start(bf16[32,48,128]{2,1,0:T(8,128)(2,1)S(1)} %get-tuple-element.7.coef_ref), channel_id=1, source_target_pairs={{0,1},{1,0},{2,3},{3,2},{4,5},{5,4},{6,7},{7,6},{8,9},{9,8},{10,11... | collective-permute-start | bytes 1179656 | tf_op jit(solution)/shard_map/ppermute | solution.py:280
  49.0 1.4 %collective-permute-start.1 = (bf16[128,768]{1,0:T(8,128)(2,1)S(1)}, bf16[128,768]{1,0:T(8,128)(2,1)S(1)}, u32[]{:S(2)}, u32[]{:S(2)}) collective-permute-start(bf16[128,768]{1,0:T(8,128)(2,1)S(1)} %bitcast.7), channel_id=1, source_target_pairs={{0,1},{1,0},{2,3},{3,2},{4,5},{5,4},{6,7},{7,6},{8,9},{9,8},{10,11... | collective-permute-start | bytes 589832 | tf_op jit(solution)/shard_map/ppermute | solution.py:280
  52.5 54.5 %copy-start = (bf16[12,1408]{1,0:T(8,128)(2,1)S(1)}, bf16[12,1408]{1,0:T(8,128)(2,1)}, u32[]{:S(2)}) copy-start(bf16[12,1408]{1,0:T(8,128)(2,1)} %win_ref.1) | copy-start | bytes 101380
  80.8 0.7 collective-permute-start.2

commit v8 on v7

--- a/solution.py
+++ b/solution.py
@@ -177,28 +177,42 @@
                 out_ref[dest] = amp[:, b * cols : (b + 1) * cols]
 
 
-def terms_kernel(blk, mask_ref, core_ref, amp_ref, other_amp_ref, ints_ref, out_ref, all_ref):
+def terms_of(blk, mask_ref, amp_ref, ints_ref, store):
     rows, cols = ints_ref.shape
-    dests, few, _ = out_ref.shape
-    half = amp_ref.shape[0]
-    side = 4
-    at = pl.multiple_of(core_ref[0] * half, half)
-    all_ref[pl.ds(at, half), :] = amp_ref[...]
-    at = pl.multiple_of((core_ref[0] ^ 1) * half, half)
-    all_ref[pl.ds(at, half), :] = other_amp_ref[...]
+    side, few = 4, 8
+    per = amp_ref.shape[0] // side
     for col in range(cols // blk):
         total = None
         for row in range(rows // blk):
             keep = mask_ref[row, col].astype(F32)
             term = keep * mm(
-                all_ref[:, row * blk : (row + 1) * blk],
+                amp_ref[:, row * blk : (row + 1) * blk],
                 ints_ref[row * blk : (row + 1) * blk, col * blk : (col + 1) * blk],
             )
             total = term if total is None else total + term
-        for dest in range(dests):
-            o, x = dest // side, dest % side
-            at = o % 2 * half + x * (half // side) + o // 2 * few
-            out_ref[dest, :, col * blk : (col + 1) * blk] = total[at : at + few].astype(BF16)
+        for x in range(side):
+            for zh in range(per // few):
+                at = x * per + zh * few
+                store(zh, x, slice(col * blk, (col + 1) * blk), total[at : at + few].astype(BF16))
+
+
+def own_terms_kernel(blk, mask_ref, amp_ref, ints_ref, out_ref):
+    def store(zh, x, cut, part):
+        out_ref[zh * 4 + x, :, cut] = part
+
+    terms_of(blk, mask_ref, amp_ref, ints_ref, store)
+
+
+def terms_kernel(blk, mask_ref, core_ref, amp_ref, ints_ref, own_ref, out_ref):
+    side = 4
+    for part in range(own_ref.shape[0]):
+        zh, x = part // side, part % side
+        out_ref[(zh * 2 + core_ref[0]) * side + x] = own_ref[part]
+
+    def store(zh, x, cut, part):
+        out_ref[(zh * 2 + (core_ref[0] ^ 1)) * side + x, :, cut] = part
+
+    terms_of(blk, mask_ref, amp_ref, ints_ref, store)
 
 
 def sum_terms_kernel(in_ref, out_ref):
@@ -352,15 +366,23 @@
     amp_here = exchange(ao_amp, ("x", "zh")).reshape(flat * few, rows)
     amp_there = swap(amp_here, "core")
 
+    blk = rows // block_mask.shape[0]
+    own_terms = pl.pallas_call(
+        functools.partial(own_terms_kernel, blk),
+        in_specs=[smem, vmem, vmem],
+        out_specs=vmem,
+        out_shape=jax.ShapeDtypeStruct((sp // 2, few, cols), BF16),
+        compiler_params=params(),
+        name="own_terms",
+    )(block_mask, amp_here, integrals)
     terms = pl.pallas_call(
-        functools.partial(terms_kernel, rows // block_mask.shape[0]),
+        functools.partial(terms_kernel, blk),
         in_specs=[smem, smem, vmem, vmem, vmem],
         out_specs=vmem,
         out_shape=jax.ShapeDtypeStruct((sp, few, cols), BF16),
-        scratch_shapes=[pltpu.VMEM((op * pairs, rows), BF16)],
         compiler_params=params(),
         name="terms",
-    )(block_mask, my_core, amp_here, amp_there, integrals)
+    )(block_mask, my_core, amp_there, integrals, own_terms)
     pieces = exchange(terms, ("y", "z", "x"))
     ladder = pl.pallas_call(
         sum_terms_kernel,

time: 110 us -> 110 us (level)
  waiting for transfers between devices: 2.38 us -> 0.96 us
    ppermute x2, waiting for transfers between devices: 2.38 us -> 0.96 us  [swap(): return lax.ppermute(array, axis, [(0, 1), (1, 0)])]
    pallas_call x1 -> x2, Pallas kernels: 2 us -> 2.81 us  [the longest x1 1.42 us: local(): pl.pallas_call(functools.partial(terms_kernel, blk), in_specs=[smem, smem...]
  transfers between devices with their start and end apart: 3 -> 3, of which waited for: 2 -> 1; matrix products, arithmetic and copies ran while one was open for 0% -> 0% of each run, Pallas kernels for 1% -> 2%
where the time goes in v8:
time: 110 us; the launch traced here: 109 us
  blocking collectives  93.6 us (85%)
  Pallas kernels  13.9 us (13%)
    all_to_all x4, blocking collectives, exchange(): return lax.all_to_all(array, axes, split_axis=0, concat_axis=0, tiled=True)  93.6 us
    pallas_call x1, Pallas kernels, local(): pl.pallas_call(functools.partial(half_kernel, steps, few), in_specs=[smem...  5.66 us
    pallas_call x1, Pallas kernels, local(): pl.pallas_call(functools.partial(out_kernel, steps, few), in_specs=[vmem,...  2.41 us
  transfers between devices with their start and end apart: 3, of which 1 were waited for; matrix products, arithmetic and copies ran while one was open for 0% of the time, Pallas kernels for 2%

profile of v8, /device:TPU:2, one launch (start us, length us, event | category | flops | bytes accessed | tf_op | source)
XLA Modules:
  0.0 109.3 jit_solution(9634124516836819656)
XLA Ops:
  0.0 0.0 slice-start
  0.0 0.0 slice-start.1
  0.0 0.0 copy-start.1
  0.0 5.7 %half.1 = bf16[32,80,128]{2,1,0:T(8,128)(2,1)} custom-call(s32[1]{0:T(128)} %bitcast.core_ref, bf16[44,32,1408]{2,1,0:T(8,128)(2,1)} %bitcast.9, bf16[12,1408]{1,0:T(8,128)(2,1)} %win_ref.1, bf16[44,2048]{1,0:T(8,128)(2,1)} %bitcast.10), custom_call_target="tpu_custom_call" | custom-call | tf_op jit(solution)/shard_map/half/pallas_call | solution.py:327
  5.7 21.1 %all_to_all.20.in_ref = bf16[32,80,128]{2,1,0:T(8,128)(2,1)S(1)} all-to-all(bf16[32,80,128]{2,1,0:T(8,128)(2,1)} %half.1), channel_id=1, replica_groups=mesh['y'=4,'z'=2,'x'=4,'zh'=4,'core'=2] {'y','z','x'}, dimensions={0} | all-to-all | bytes 1310720 | tf_op jit(solution)/shard_map/all_to_all | solution.py:304
  26.8 0.2 unpack.1
  27.0 0.1 collective-permute-start
  27.1 0.8 own_amp.1.own_ref
  27.9 0.9 collective-permute-done.coef_ref.other_coef_ref
  28.8 0.8 amp.1
  29.6 19.4 %all_to_all.21 = bf16[16,8,768]{2,1,0:T(8,128)(2,1)S(1)} all-to-all(bf16[16,8,768]{2,1,0:T(8,128)(2,1)S(1)} %amp.1), channel_id=1, replica_groups=mesh['y'=4,'z'=2,'x'=4,'zh'=4,'core'=2] {'x','zh'}, dimensions={0} | all-to-all | bytes 393216 | tf_op jit(solution)/shard_map/all_to_all | solution.py:304
  49.0 0.0 collective-permute-start.1
  49.0 0.0 slice-done
  49.0 0.0 slice-done.1
  49.0 0.0 copy-done.1
  49.0 1.4 %own_terms.1.own_ref = bf16[16,8,3072]{2,1,0:T(8,128)(2,1)S(1)} custom-call(s32[3,12]{1,0:T(4,128)S(1)} %copy-done.1, bf16[128,768]{1,0:T(8,128)(2,1)S(1)} %bitcast.8, bf16[768,3072]{1,0:T(8,128)(2,1)S(1)} %bitcast.6), custom_call_target="tpu_custom_call" | custom-call | tf_op jit(solution)/shard_map/own_terms/pallas_call | solution.py:370
  50.4 0.0 collective-permute-done.1.amp_ref
  50.4 1.4 %terms.1 = bf16[32,8,3072]{2,1,0:T(8,128)(2,1)S(1)} custom-call(s32[3,12]{1,0:T(4,128)S(1)} %copy-done.1, s32[1]{0:T(128)} %bitcast.core_ref, bf16[128,768]{1,0:T(8,128)(2,1)S(1)} %collective-permute-done.1.amp_ref, bf16[768,3072]{1,0:T(8,128)(2,1)S(1)} %bitcast.6, bf16[16,8,3072]{2,1,0:T(8,128)(2,1)S(1)} %own_terms.1.own_ref), custom_call_target="tpu_custom_call" | custom-call | tf_op jit(solution)/shard_map/terms/pallas_call | solution.py:378
  51.9 0.0 copy-start
  51.9 28.5 %all_to_all.22.in_ref = bf16[32,8,3072]{2,1,0:T(8,128)(2,1)S(1)} all-to-all(bf16[32,8,3072]{2,1,0:T(8,128)(2,1)S(1)} %terms.1), channel_id=1, replica_groups=mesh['y'=4,'z'=2,'x'=4,'zh'=4,'core'=2] {'y','z','x'}, dimensions={0} | all-to-all | bytes 3145728 | tf_op jit(solution)/shard_map/all_to_all | solution.py:304
  80.4 0.2 sum_terms.1
  80.6 0.7 collective-permute-start.2
  81.3 0.0 collective-permute-done.2.lad_ref
  81.3 1.1 forward.1
  82.4 24.5 %all_to_all.23.fwd_ref = bf16[32,40,128]{2,1,0:T(8,128)(2,1)S(1)} all-to-all(bf16[32,40,128]{2,1,0:T(8,128)(2,1)S(1)} %forward.1), channel_id=1, replica_groups=mesh['y'=4,'z'=2,'x'=4,'zh'=4,'core'=2] {'y','z','x'}, dimensions={0} | all-to-all | bytes 655360 | tf_op jit(solution)/shard_map/all_to_all | solution.py:304
  106.9 0.0 copy-done
  106.9 2.4 %out.1 = bf16[44,32,1408]{2,1,0:T(8,128)(2,1)} custom-call(bf16[32,40,128]{2,1,0:T(8,128)(2,1)S(1)} %all_to_all.23.fwd_ref, bf16[12,1408]{1,0:T(8,128)(2,1)S(1)} %copy-done), custom_call_target="tpu_custom_call" | custom-call | tf_op jit(solution)/shard_map/out/pallas_call | solution.py:404
  (1 shorter events, 0.0 us)
Async XLA Ops:
  0.0 49.0 %slice-start = ((s8[4718592]{0:T(1024)(128)(4,1)}), s8[4194304]{0:T(1024)(128)(4,1)S(1)}, s32[]{:S(2)}) async-start(s8[4718592]{0:T(1024)(128)(4,1)} %bitcast.5), calls=%async_computation.4 | async-start | bytes 8388608
  0.0 49.0 %slice-start.1 = ((s8[4718592]{0:T(1024)(128)(4,1)}), s8[524288]{0:T(1024)(128)(4,1)S(1)}, s32[]{:S(2)}) async-start(s8[4718592]{0:T(1024)(128)(4,1)} %bitcast.5), calls=%async_computation.5 | async-start | bytes 1048576
  0.0 49.0 %copy-start.1 = (s32[3,12]{1,0:T(4,128)S(1)}, s32[3,12]{1,0:T(4,128)}, u32[]{:S(2)}) copy-start(s32[3,12]{1,0:T(4,128)} %mask_ref.3) | copy-start | bytes 436
  27.0 1.8 %collective-permute-start = (bf16[32,48,128]{2,1,0:T(8,128)(2,1)S(1)}, bf16[32,48,128]{2,1,0:T(8,128)(2,1)S(1)}, u32[]{:S(2)}, u32[]{:S(2)}) collective-permute-start(bf16[32,48,128]{2,1,0:T(8,128)(2,1)S(1)} %get-tuple-element.7.coef_ref), channel_id=1, source_target_pairs={{0,1},{1,0},{2,3},{3,2},{4,5},{5,4},{6,7},{7,6},{8,9},{9,8},{10,11... | collective-permute-start | bytes 1179656 | tf_op jit(solution)/shard_map/ppermute | solution.py:294
  49.0 1.4 %collective-permute-start.1 = (bf16[128,768]{1,0:T(8,128)(2,1)S(1)}, bf16[128,768]{1,0:T(8,128)(2,1)S(1)}, u32[]{:S(2)}, u32[]{:S(2)}) collective-permute-start(bf16[128,768]{1,0:T(8,128)(2,1)S(1)} %bitcast.7), channel_id=1, source_target_pairs={{0,1},{1,0},{2,3},{3,2},{4,5},{5,4},{6,7},{7,6},{8,9},{9,8},{10,11... | collective-permute-start | bytes 589832 | tf_op jit(solution)/shard_map/ppermute | solution.py:294
  51.9 55.0 %copy-start = (bf16[12,1408]{1,0:T(8,128)(2,1)S(1)}, bf16[12,1408]{1,0:T(8,128)(2,1)}, u32[]{:S(2)}) copy-start(bf16[12,1408]{1,0:T(8,128)(2,1)} %win_ref.1) | copy-start | bytes 101380
  80.6 0.7 collective-permute-start.2

commit v9 on v8

--- a/solution.py
+++ b/solution.py
@@ -63,7 +63,7 @@
     free = width - cols
     virt = total // steps
     rows = virt * pairs
-    ahead = 3
+    ahead = steps
     copies = [
         pltpu.make_async_copy(
             amp_hbm.at[step * virt : (step + 1) * virt],
@@ -139,21 +139,21 @@
     return lax.dot_general(pick, wide, LANES, preferred_element_type=F32)[:few].astype(BF16)
 
 
-def unpack_kernel(cols, last, in_ref, coef_ref, half_ref):
+def unpack_kernel(cols, last, half, in_ref, out_ref):
     parts, both, mus = in_ref.shape
     packed = both // 2
     free = mus - cols
-    whole = in_ref[...].astype(F32)
-    rest = whole[:, packed:, cols:]
-    none = jnp.zeros((parts, coef_ref.shape[1] - packed - last, mus), F32)
     count = mus // free
-    coef = [rest[:, i * last : (i + 1) * last] for i in range(count)]
-    coef = jnp.concatenate([whole[:, :packed], jnp.concatenate(coef, axis=2), none], axis=1)
-    coef_ref[...] = coef.astype(BF16)
-    half = [rest[:, i * last : (i + 1) * last] for i in range(count, count + cols // free)]
-    half.append(jnp.zeros((parts, last, free), F32))
-    half = jnp.concatenate([whole[:, packed:], jnp.concatenate(half, axis=2), none], axis=1)
-    half_ref[...] = half.astype(BF16)
+    rest = in_ref[...].astype(F32)[:, packed:, cols:]
+    if half:
+        main = in_ref[...].astype(F32)[:, packed:]
+        tail = [rest[:, i * last : (i + 1) * last] for i in range(count, count + cols // free)]
+        tail.append(jnp.zeros((parts, last, free), F32))
+    else:
+        main = in_ref[...].astype(F32)[:, :packed]
+        tail = [rest[:, i * last : (i + 1) * last] for i in range(count)]
+    none = jnp.zeros((parts, out_ref.shape[1] - packed - last, mus), F32)
+    out_ref[...] = jnp.concatenate([main, jnp.concatenate(tail, axis=2), none], axis=1).astype(BF16)
 
 
 def own_amp_kernel(nuw, half_ref, coef_ref, out_ref):
@@ -341,12 +341,15 @@
         name="half",
     )(my_core, amp, window_coef, coef)
     chunk = exchange(sent, ("y", "z", "x"))
-    own_coef, half = pl.pallas_call(
-        functools.partial(unpack_kernel, nuw * few, virt - packed),
-        out_shape=[jax.ShapeDtypeStruct((sp, padded, width), BF16)] * 2,
-        compiler_params=params(),
-        name="unpack",
-    )(chunk)
+    own_coef, half = [
+        pl.pallas_call(
+            functools.partial(unpack_kernel, nuw * few, virt - packed, which),
+            out_shape=jax.ShapeDtypeStruct((sp, padded, width), BF16),
+            compiler_params=params(),
+            name="unpack",
+        )(chunk)
+        for which in (False, True)
+    ]
     other_coef = swap(own_coef, "core")
     flat = sizes["x"] * sizes["zh"]
     own_amp = pl.pallas_call(

time: 110 us -> 110 us (level)
  no operation moved by 1% of the time
where the time goes in v9:
time: 110 us; the launch traced here: 109 us
  blocking collectives  93.8 us (85%)
  Pallas kernels  14 us (13%)
    all_to_all x4, blocking collectives, exchange(): return lax.all_to_all(array, axes, split_axis=0, concat_axis=0, tiled=True)  93.8 us
    pallas_call x1, Pallas kernels, local(): pl.pallas_call(functools.partial(half_kernel, steps, few), in_specs=[smem...  5.52 us
    pallas_call x1, Pallas kernels, local(): pl.pallas_call(functools.partial(out_kernel, steps, few), in_specs=[vmem,...  2.41 us
  transfers between devices with their start and end apart: 3, of which 1 were waited for; matrix products, arithmetic and copies ran while one was open for 0% of the time, Pallas kernels for 2%

profile of v9, /device:TPU:2, one launch (start us, length us, event | category | flops | bytes accessed | tf_op | source)
XLA Modules:
  0.0 109.5 jit_solution(742493192549588350)
XLA Ops:
  0.0 5.5 %half.1 = bf16[32,80,128]{2,1,0:T(8,128)(2,1)} custom-call(s32[1]{0:T(128)} %bitcast.core_ref, bf16[44,32,1408]{2,1,0:T(8,128)(2,1)} %bitcast.7, bf16[12,1408]{1,0:T(8,128)(2,1)} %win_ref.1, bf16[44,2048]{1,0:T(8,128)(2,1)} %bitcast.8), custom_call_target="tpu_custom_call" | custom-call | tf_op jit(solution)/shard_map/half/pallas_call | solution.py:327
  5.5 0.0 copy-start
  5.5 0.0 copy-start.2
  5.6 21.4 %all_to_all.20.in_ref = bf16[32,80,128]{2,1,0:T(8,128)(2,1)S(1)} all-to-all(bf16[32,80,128]{2,1,0:T(8,128)(2,1)} %half.1), channel_id=1, replica_groups=mesh['y'=4,'z'=2,'x'=4,'zh'=4,'core'=2] {'y','z','x'}, dimensions={0} | all-to-all | bytes 1310720 | tf_op jit(solution)/shard_map/all_to_all | solution.py:304
  27.0 0.1 unpack.2.coef_ref
  27.1 0.1 collective-permute-start
  27.2 0.1 unpack.3.half_ref
  27.3 0.8 own_amp.1.own_ref
  28.1 0.8 collective-permute-done.coef_ref.other_coef_ref
  28.9 0.8 amp.1
  29.7 19.4 %all_to_all.21 = bf16[16,8,768]{2,1,0:T(8,128)(2,1)S(1)} all-to-all(bf16[16,8,768]{2,1,0:T(8,128)(2,1)S(1)} %amp.1), channel_id=1, replica_groups=mesh['y'=4,'z'=2,'x'=4,'zh'=4,'core'=2] {'x','zh'}, dimensions={0} | all-to-all | bytes 393216 | tf_op jit(solution)/shard_map/all_to_all | solution.py:304
  49.1 0.0 collective-permute-start.1
  49.1 0.0 copy-done
  49.1 0.0 copy-done.2
  49.1 1.4 %own_terms.1.own_ref = bf16[16,8,3072]{2,1,0:T(8,128)(2,1)S(1)} custom-call(s32[3,12]{1,0:T(4,128)S(1)} %copy-done.2, bf16[128,768]{1,0:T(8,128)(2,1)S(1)} %bitcast.6, bf16[768,3072]{1,0:T(8,128)(2,1)S(1)} %copy-done), custom_call_target="tpu_custom_call" | custom-call | tf_op jit(solution)/shard_map/own_terms/pallas_call | solution.py:373
  50.5 0.0 collective-permute-done.1.amp_ref
  50.5 1.5 %terms.1 = bf16[32,8,3072]{2,1,0:T(8,128)(2,1)S(1)} custom-call(s32[3,12]{1,0:T(4,128)S(1)} %copy-done.2, s32[1]{0:T(128)} %bitcast.core_ref, bf16[128,768]{1,0:T(8,128)(2,1)S(1)} %collective-permute-done.1.amp_ref, bf16[768,3072]{1,0:T(8,128)(2,1)S(1)} %copy-done, bf16[16,8,3072]{2,1,0:T(8,128)(2,1)S(1)} %own_terms.1.own_ref), custom_call_target="tpu_custom_call" | custom-call | tf_op jit(solution)/shard_map/terms/pallas_call | solution.py:381
  52.0 0.0 copy-start.1
  52.0 28.5 %all_to_all.22.in_ref = bf16[32,8,3072]{2,1,0:T(8,128)(2,1)S(1)} all-to-all(bf16[32,8,3072]{2,1,0:T(8,128)(2,1)S(1)} %terms.1), channel_id=1, replica_groups=mesh['y'=4,'z'=2,'x'=4,'zh'=4,'core'=2] {'y','z','x'}, dimensions={0} | all-to-all | bytes 3145728 | tf_op jit(solution)/shard_map/all_to_all | solution.py:304
  80.6 0.2 sum_terms.1
  80.8 0.7 collective-permute-start.2
  81.4 0.0 collective-permute-done.2.lad_ref
  81.4 1.1 forward.1
  82.5 24.5 %all_to_all.23.fwd_ref = bf16[32,40,128]{2,1,0:T(8,128)(2,1)S(1)} all-to-all(bf16[32,40,128]{2,1,0:T(8,128)(2,1)S(1)} %forward.1), channel_id=1, replica_groups=mesh['y'=4,'z'=2,'x'=4,'zh'=4,'core'=2] {'y','z','x'}, dimensions={0} | all-to-all | bytes 655360 | tf_op jit(solution)/shard_map/all_to_all | solution.py:304
  107.1 0.0 copy-done.1
  107.1 2.4 %out.1 = bf16[44,32,1408]{2,1,0:T(8,128)(2,1)} custom-call(bf16[32,40,128]{2,1,0:T(8,128)(2,1)S(1)} %all_to_all.23.fwd_ref, bf16[12,1408]{1,0:T(8,128)(2,1)S(1)} %copy-done.1), custom_call_target="tpu_custom_call" | custom-call | tf_op jit(solution)/shard_map/out/pallas_call | solution.py:407
Async XLA Ops:
  5.5 43.5 %copy-start = (bf16[768,3072]{1,0:T(8,128)(2,1)S(1)}, bf16[768,3072]{1,0:T(8,128)(2,1)}, u32[]{:S(2)}) copy-start(bf16[768,3072]{1,0:T(8,128)(2,1)} %ints_ref.3) | copy-start | bytes 14155780
  5.5 43.5 %copy-start.2 = (s32[3,12]{1,0:T(4,128)S(1)}, s32[3,12]{1,0:T(4,128)}, u32[]{:S(2)}) copy-start(s32[3,12]{1,0:T(4,128)} %mask_ref.3) | copy-start | bytes 436
  27.1 1.8 %collective-permute-start = (bf16[32,48,128]{2,1,0:T(8,128)(2,1)S(1)}, bf16[32,48,128]{2,1,0:T(8,128)(2,1)S(1)}, u32[]{:S(2)}, u32[]{:S(2)}) collective-permute-start(bf16[32,48,128]{2,1,0:T(8,128)(2,1)S(1)} %unpack.2.coef_ref), channel_id=1, source_target_pairs={{0,1},{1,0},{2,3},{3,2},{4,5},{5,4},{6,7},{7,6},{8,9},{9,8},{10,11... | collective-permute-start | bytes 1179656 | tf_op jit(solution)/shard_map/ppermute | solution.py:294
  49.1 1.5 %collective-permute-start.1 = (bf16[128,768]{1,0:T(8,128)(2,1)S(1)}, bf16[128,768]{1,0:T(8,128)(2,1)S(1)}, u32[]{:S(2)}, u32[]{:S(2)}) collective-permute-start(bf16[128,768]{1,0:T(8,128)(2,1)S(1)} %bitcast.5), channel_id=1, source_target_pairs={{0,1},{1,0},{2,3},{3,2},{4,5},{5,4},{6,7},{7,6},{8,9},{9,8},{10,11... | collective-permute-start | bytes 589832 | tf_op jit(solution)/shard_map/ppermute | solution.py:294
  52.0 55.1 %copy-start.1 = (bf16[12,1408]{1,0:T(8,128)(2,1)S(1)}, bf16[12,1408]{1,0:T(8,128)(2,1)}, u32[]{:S(2)}) copy-start(bf16[12,1408]{1,0:T(8,128)(2,1)} %win_ref.1) | copy-start | bytes 101380
  80.8 0.7 collective-permute-start.2
